TPU v7x, 128 devices: a whole 4x4x4 slice. The times are simulated.
128 devices in a mesh: row: 16 (over z, x), col: 8 (over y, core).
Axes of the slice: x: 4, y: 4, z: 4, core: 2. Of those that a mesh axis runs over, the one named last changes fastest.
Arguments:
- density: float32 [16, 80, 128, 128], P('row', 'col'), may hold values from -0.3 to 0.3
- hamiltonian: float32 [16, 80, 128, 128], P('row', 'col'), may hold values from -0.3 to 0.3
- block_rows: int32 [16, 80], P('row', 'col'), may hold values from 0 to 511, as said below
- block_cols: int32 [16, 80], P('row', 'col'), may hold values from 0 to 511, as said below
- left_index: int32 [16, 80, 3], P('row', 'col'), may hold values from -1 to 79, as said below
- right_index: int32 [16, 80, 3], P('row', 'col'), may hold values from -1 to 159, as said below
Outputs:
- new_density: float32 [16, 80, 128, 128], P('row', 'col')
- energy_weighted: float32 [16, 80, 128, 128], P('row', 'col')
Inputs may be any that keep to these rules, and one draw needn't show every extreme that they name: -1 marks an empty term and live terms come first in each list; a live term pairs the stored block (i, j) of the left matrix with the stored block (j, k) of the right matrix, where (i, k) is the stored block that it sums into; a list holds all such pairs; a term is live in left_index exactly where it is in right_index; the left block of a live term of device (r, c) is stored on device (r, c - 1), (r, c) or (r, c + 1), column indices counted round. `right_index`: as for left_index. `block_rows`: the block row of a block of device (r, c) leaves the remainder r when divided by 16; the pattern is symmetric, every block row has its diagonal block stored, and the stored blocks of one device are distinct. `block_cols`: a block column k of a block of device (r, c) has (k // 16) % 8 equal to c.
All inputs are finite; a program needn't handle non-finite values.
Results may differ from a plain program's by a relative error of at most 0.0003.
Values sent between devices are 32-bit elements; how exact they have to be, the bound alone decides.
A program may use at most 128 MiB of HBM per device.

v0:
```python
import jax
import jax.numpy as jnp
from jax import lax
from jax.sharding import PartitionSpec as P


def extended(array, sides, width):
    for axis, dim in sides:
        size, length = (lax.axis_size(axis), array.shape[dim])
        up = [(i, (i + 1) % size) for i in range(size)]
        down = [(j, i) for i, j in up]
        last = lax.slice_in_dim(array, length - width, length, axis=dim)
        leading = lax.slice_in_dim(array, 0, width, axis=dim)
        before = lax.ppermute(last, axis, up)
        after = lax.ppermute(leading, axis, down)
        array = jnp.concatenate([before, array, after], axis=dim)
    return array


def stack_product(row_panel, col_panel, left_part, right_part):
    live_terms = ((left_part >= 0) & (right_part >= 0)).astype(jnp.float32)
    left_blocks = jnp.take(row_panel, jnp.maximum(left_part, 0), axis=0)
    right_blocks = jnp.take(col_panel, jnp.maximum(right_part, 0), axis=0)
    left_blocks = left_blocks * live_terms[:, :, None, None]
    return jnp.einsum("stij,stjk->sik", left_blocks, right_blocks, precision=lax.Precision.HIGHEST)


def flatten_column(panel):
    return panel.reshape(panel.shape[0] * panel.shape[1], panel.shape[2], panel.shape[3])


def diag_trace(blocks, on_diag):
    return jnp.sum(jnp.where(on_diag, jnp.trace(blocks, axis1=-2, axis2=-1), jnp.float32(0.0)))


def near_index(left_part, slot_count, col_count, col_id):
    owner = jnp.maximum(left_part, 0) // slot_count
    within = jnp.maximum(left_part, 0) % slot_count
    place = (owner - col_id + 1) % col_count
    return jnp.where(left_part >= 0, place * slot_count + within, -1)


def shards(density, hamiltonian, block_rows, block_cols, left_index, right_index):
    on_diag = block_rows[0] == block_cols[0]
    slot_count = density.shape[1]
    left_part = near_index(left_index[0], slot_count, lax.axis_size("col"), lax.axis_index("col"))
    right_part = right_index[0]
    own_density = density[0]
    row_panel = extended(density, (("col", 1),), slot_count)[0]
    col_density = flatten_column(lax.all_gather(density, "row", axis=0, tiled=True))
    square = stack_product(row_panel, col_density, left_part, right_part)
    square_local = square[None]
    trace_one = diag_trace(own_density, on_diag)
    trace_two = diag_trace(square, on_diag)
    trace_one, trace_two = lax.psum((trace_one, trace_two), ("row", "col"))
    row_square = extended(square_local, (("col", 1),), slot_count)[0]
    col_square, col_energy = (
        lax.all_gather(square_local, "row", axis=0, tiled=True),
        lax.all_gather(hamiltonian, "row", axis=0, tiled=True),
    )
    col_square = flatten_column(col_square)
    col_energy = flatten_column(col_energy)
    third_power = stack_product(row_square, col_density, left_part, right_part)
    fourth = stack_product(row_square, col_square, left_part, right_part)
    energy_weighted = stack_product(row_square, col_energy, left_part, right_part)
    trace_three = diag_trace(third_power, on_diag)
    trace_four = diag_trace(fourth, on_diag)
    trace_three, trace_four = lax.psum((trace_three, trace_four), ("row", "col"))
    trace_f = 4.0 * trace_three - 3.0 * trace_four
    trace_g = trace_four - 2.0 * trace_three + trace_two
    gamma_term = jnp.clip((trace_one - trace_f) / jnp.maximum(jnp.abs(trace_g), 1.0), 0.0, 6.0)
    new_density = (
        4.0 * third_power - 3.0 * fourth + gamma_term * (fourth - 2.0 * third_power + square)
    )
    return (new_density[None], energy_weighted[None])


def solution(mesh):
    in_specs = (
        P("row", "col", None, None),
        P("row", "col", None, None),
        P("row", "col"),
        P("row", "col"),
        P("row", "col", None),
        P("row", "col", None),
    )
    out_specs = (P("row", "col", None, None), P("row", "col", None, None))
    return jax.shard_map(shards, mesh=mesh, in_specs=in_specs, out_specs=out_specs, check_vma=False)
```

profile of v0, /device:TPU:1, one launch (start us, length us, event | category | flops | bytes accessed | tf_op | source)
XLA Modules:
  0.0 350.1 jit_solution(12739911191070185177)
XLA Ops:
  7.2 0.0 all-gather.5.cloned.1.call-start
  7.2 0.7 all-gather.5.cloned.1.call-update
  7.9 0.0 all-gather.7.cloned.1.call-start
  7.9 0.7 all-gather.7.cloned.1.call-update
  8.6 0.0 all-gather.9.cloned.1.call-start
  8.7 1.4 collective-permute-start.1
  10.1 1.3 collective-permute-start
  11.4 0.7 broadcast_remainder_fusion
  12.1 0.7 broadcast_compare_fusion.2
  12.8 0.1 copy.32
  12.9 0.1 reshape.139
  13.0 0.7 broadcast_maximum_fusion.1
  13.7 0.1 copy.35
  13.8 0.1 reshape.143
  13.9 0.7 broadcast_compare_fusion.1
  14.6 0.1 copy.33
  14.7 0.1 copy.30
  14.8 0.1 copy.34
  14.9 5.2 %collective-permute-done.1 = f32[1,10,128,128]{3,2,1,0:T(8,128)S(1)} collective-permute-done((f32[1,10,128,128]{3,2,1,0:T(8,128)}, f32[1,10,128,128]{3,2,1,0:T(8,128)S(1)}, u32[]{:S(2)}, u32[]{:S(2)}) %collective-permute-start.1) | collective-permute-done | bytes 655392 | tf_op jit(solution)/shard_map/ppermute | solution.py:15
  20.2 0.0 collective-permute-done
  20.2 1.2 maximum_bitcast_fusion
  21.4 1.9 gather_fusion
  23.4 70.5 %all-gather.5.cloned.1.call-done = f32[16,10,128,128]{3,2,1,0:T(8,128)} async-done(((f32[1,10,128,128]{3,2,1,0:T(8,128)}), f32[16,10,128,128]{3,2,1,0:T(8,128)}) %all-gather.5.cloned.1.call-update) | async-done | bytes 10485776 | tf_op jit(solution)/shard_map/all_gather | solution.py:50
  93.9 4.6 %gather_fusion.1 = f32[30,128,128]{2,1,0:T(8,128)S(1)} fusion(f32[160,128,128]{2,1,0:T(8,128)} %bitcast.92, s32[1024]{0:T(1024)S(1)} %pad_clamp_fusion), kind=kCustom, calls=%fused_computation.1.clone | custom fusion | bytes 3932280 | tf_op jit(solution)/shard_map/jit(_take)/gather | solution.py:23
  98.6 5.3 %fusion.4 = f32[10,128,128,1]{2,1,3,0:T(8,128)} fusion(f32[10,3,128,128]{3,2,1,0:T(8,128)} %bitcast.89, f32[10,3,128,128]{3,2,1,0:T(8,128)S(1)} %bitcast.82, f32[10,3]{1,0:T(8,128)S(1)} %copy.33, pred[10,3]{1,0:T(8,128)(4,1)S(1)} %copy.30, pred[10,3]{1,0:T(8,128)(4,1)S(1)} %copy.34), kind=kOutput, calls=%fused_computation.13 | convolution fusion | flops 756449280 | bytes 4587700 | tf_op jit(solution)/shard_map/stij,stjk->sik/dot_general | solution.py:25
  103.9 0.0 copy-done
  103.9 0.0 all-gather.9.cloned.1.call-update
  104.0 0.7 collective-permute-start.3
  104.6 1.1 collective-permute-start.2
  105.8 70.4 %all-gather.7.cloned.1.call-done = f32[16,10,128,128]{3,2,1,0:T(8,128)} async-done(((f32[1,10,128,128]{3,2,1,0:T(8,128)}), f32[16,10,128,128]{3,2,1,0:T(8,128)}) %all-gather.7.cloned.1.call-update) | async-done | bytes 10485776 | tf_op jit(solution)/shard_map/all_gather | solution.py:59
  176.2 6.0 %gather_fusion.4 = f32[30,128,128]{2,1,0:T(8,128)} fusion(f32[160,128,128]{2,1,0:T(8,128)} %bitcast.91, s32[1024]{0:T(1024)S(1)} %pad_clamp_fusion), kind=kCustom, calls=%fused_computation.4.clone | custom fusion | bytes 3932280 | tf_op jit(solution)/shard_map/jit(_take)/gather | solution.py:23
  182.2 0.0 collective-permute-done.3
  182.2 0.0 collective-permute-done.2
  182.2 0.0 copy-done.2
  182.2 1.4 maximum_bitcast_fusion.1
  183.6 2.2 gather_fusion.2
  185.8 4.6 %fusion.14 = f32[1,10,128,128]{3,2,1,0:T(8,128)} fusion(f32[10,3,128,128]{3,2,1,0:T(8,128)} %bitcast.88, f32[10,3,128,128]{3,2,1,0:T(8,128)S(1)} %bitcast.79, f32[10,3]{1,0:T(8,128)S(1)} %copy.33, pred[10,3]{1,0:T(8,128)(4,1)S(1)} %copy.30, pred[10,3]{1,0:T(8,128)(4,1)S(1)} %copy.34), kind=kOutput, calls=%fused_computation.19 | convolution fusion | flops 756449280 | bytes 4587700 | tf_op jit(solution)/shard_map/stij,stjk->sik/dot_general | solution.py:25
  190.5 68.6 %all-gather.9.cloned.1.call-done = f32[160,128,128]{2,1,0:T(8,128)} async-done(((f32[10,128,128]{2,1,0:T(8,128)}), f32[160,128,128]{2,1,0:T(8,128)}) %all-gather.9.cloned.1.call-update) | async-done | bytes 10485776 | tf_op jit(solution)/shard_map/all_gather | solution.py:58
  259.1 5.9 %gather_fusion.3 = f32[30,128,128]{2,1,0:T(8,128)} fusion(f32[160,128,128]{2,1,0:T(8,128)} %all-gather.9.cloned.1.call-done, s32[1024]{0:T(1024)S(1)} %pad_clamp_fusion), kind=kCustom, calls=%fused_computation.3.clone | custom fusion | bytes 3932280 | tf_op jit(solution)/shard_map/jit(_take)/gather | solution.py:23
  265.0 4.0 %fusion.11 = f32[10,128,128]{2,1,0:T(8,128)S(1)} fusion(f32[10,3,128,128]{3,2,1,0:T(8,128)} %bitcast.90, f32[10,3,128,128]{3,2,1,0:T(8,128)S(1)} %bitcast.80, f32[10,3]{1,0:T(8,128)S(1)} %copy.33, pred[10,3]{1,0:T(8,128)(4,1)S(1)} %copy.30, pred[10,3]{1,0:T(8,128)(4,1)S(1)} %copy.34), kind=kOutput, calls=%fused_computation.18 | convolution fusion | flops 756449280 | bytes 4587700 | tf_op jit(solution)/shard_map/stij,stjk->sik/dot_general | solution.py:25
  269.0 0.0 copy-done.1
  269.0 0.0 copy-done.3
  269.0 0.0 copy-start.4
  269.0 0.0 copy-start.5
  269.0 3.2 select_reduce_fusion
  272.2 0.7 fusion.45
  272.9 64.9 %all-reduce = (f32[]{:T(128)}, f32[]{:T(128)}, f32[]{:T(128)}, f32[]{:T(128)}) all-reduce(f32[]{:T(128)} %get-tuple-element.11, f32[]{:T(128)} %get-tuple-element.9, f32[]{:T(128)} %get-tuple-element.10, f32[]{:T(128)} %get-tuple-element.8), channel_id=1, replica_groups=mesh['row'=16,'col'=8] {'row','col'}, use_global_device_ids=true, to_apply=%region_2.5 | all-reduce | flops 4 | bytes 32 | tf_op jit(solution)/shard_map/psum | solution.py:55
  341.5 2.1 add_bitcast_fusion
  (14 shorter events, 0.1 us)
Async XLA Ops:
  7.2 86.8 %all-gather.5.cloned.1.call-start = ((), (), s32[]{:S(2)}) async-start(), calls=%async_computation | async-start | bytes 11141120 | tf_op jit(solution)/shard_map/all_gather | solution.py:50
  7.9 168.3 %all-gather.7.cloned.1.call-start = ((), (), s32[]{:S(2)}) async-start(), calls=%async_computation.1 | async-start | bytes 11141120 | tf_op jit(solution)/shard_map/all_gather | solution.py:59
  8.6 250.4 %all-gather.9.cloned.1.call-start = ((), (), s32[]{:S(2)}) async-start(), calls=%async_computation.2 | async-start | bytes 11141120 | tf_op jit(solution)/shard_map/all_gather | solution.py:58
  8.7 11.5 %collective-permute-start.1 = (f32[1,10,128,128]{3,2,1,0:T(8,128)}, f32[1,10,128,128]{3,2,1,0:T(8,128)S(1)}, u32[]{:S(2)}, u32[]{:S(2)}) collective-permute-start(f32[1,10,128,128]{3,2,1,0:T(8,128)} %param.10), channel_id=1, source_target_pairs={{1,0},{2,1},{3,2},{4,3},{5,4},{6,5},{7,6},{0,7},{9,8},{10,9},{11,1... | collective-permute-start | bytes 1966088 | tf_op jit(solution)/shard_map/ppermute | solution.py:15
  10.1 10.0 %collective-permute-start = (f32[1,10,128,128]{3,2,1,0:T(8,128)}, f32[1,10,128,128]{3,2,1,0:T(8,128)S(1)}, u32[]{:S(2)}, u32[]{:S(2)}) collective-permute-start(f32[1,10,128,128]{3,2,1,0:T(8,128)} %param.10), channel_id=1, source_target_pairs={{0,1},{1,2},{2,3},{3,4},{4,5},{5,6},{6,7},{7,0},{8,9},{9,10},{10,1... | collective-permute-start | bytes 1966088 | tf_op jit(solution)/shard_map/ppermute | solution.py:14
  98.6 5.4 %copy-start = (f32[30,128,128]{2,1,0:T(8,128)}, f32[30,128,128]{2,1,0:T(8,128)S(1)}, u32[]{:S(2)}) copy-start(f32[30,128,128]{2,1,0:T(8,128)S(1)} %gather_fusion.1) | copy-start | bytes 5898244
  104.0 78.2 %collective-permute-start.3 = (f32[1,10,128,128]{3,2,1,0:T(8,128)}, f32[1,10,128,128]{3,2,1,0:T(8,128)S(1)}, u32[]{:S(2)}, u32[]{:S(2)}) collective-permute-start(f32[1,10,128,128]{3,2,1,0:T(8,128)} %bitcast.85), channel_id=1, source_target_pairs={{1,0},{2,1},{3,2},{4,3},{5,4},{6,5},{7,6},{0,7},{9,8},{10,9},{11,1... | collective-permute-start | bytes 1966088 | tf_op jit(solution)/shard_map/ppermute | solution.py:15
  104.6 77.6 %collective-permute-start.2 = (f32[1,10,128,128]{3,2,1,0:T(8,128)}, f32[1,10,128,128]{3,2,1,0:T(8,128)S(1)}, u32[]{:S(2)}, u32[]{:S(2)}) collective-permute-start(f32[1,10,128,128]{3,2,1,0:T(8,128)} %bitcast.86), channel_id=1, source_target_pairs={{0,1},{1,2},{2,3},{3,4},{4,5},{5,6},{6,7},{7,0},{8,9},{9,10},{10,1... | collective-permute-start | bytes 1966088 | tf_op jit(solution)/shard_map/ppermute | solution.py:14
  176.2 6.0 %copy-start.2 = (f32[10,128,128,1]{2,1,3,0:T(8,128)S(1)}, f32[10,128,128,1]{2,1,3,0:T(8,128)}, u32[]{:S(2)}) copy-start(f32[10,128,128,1]{2,1,3,0:T(8,128)} %fusion.4) | copy-start | bytes 1966084
  265.0 4.0 %copy-start.1 = (f32[30,128,128]{2,1,0:T(8,128)S(1)}, f32[30,128,128]{2,1,0:T(8,128)}, u32[]{:S(2)}) copy-start(f32[30,128,128]{2,1,0:T(8,128)} %copy-done) | copy-start | bytes 5898244
  265.0 4.0 %copy-start.3 = (f32[1,10,128,128]{3,2,1,0:T(8,128)S(1)}, f32[1,10,128,128]{3,2,1,0:T(8,128)}, u32[]{:S(2)}) copy-start(f32[1,10,128,128]{3,2,1,0:T(8,128)} %param.10) | copy-start | bytes 1966084
  269.0 3.2 copy-start.4
  269.0 3.2 copy-start.5
Sparse Core Ops, SparseCore 0:
  10.1 83.7 all-gather.4
  96.0 80.0 all-gather.6
  178.9 80.0 all-gather.8
where the time goes:
time: 351 us; the launch traced here: 350 us
  waiting for transfers between devices  216 us (62%)
  blocking collectives  64.9 us (18%)
  local copies, waits for them, and re-layouts  21.4 us (6%)
  between operations  17.6 us (5%)
  matrix products  17.1 us (5%)
  other arithmetic  8.27 us (2%)
  starting transfers between devices  4.64 us (1%)
    all_gather x1, waiting for transfers between devices, shards(): lax.all_gather(density, 'row', axis=0, tiled=True)  70.5 us
    all_gather x1, waiting for transfers between devices, shards(): lax.all_gather(hamiltonian, 'row', axis=0, tiled=True)  70.4 us
    all_gather x1, waiting for transfers between devices, shards(): lax.all_gather(square_local, 'row', axis=0, tiled=True)  68.6 us
    psum x1, blocking collectives, shards(): trace_one, trace_two = lax.psum((trace_one, trace_two), ('row', 'col'))  64.9 us
    dot_general x4, matrix products, stack_product(): jnp.einsum('stij,stjk->sik', left_blocks, right_blocks, precision=lax.Pre...  17.1 us
    gather x3, local copies, waits for them, and re-layouts, stack_product(): right_blocks = jnp.take(col_panel, jnp.maximum(right_part, 0), axis=0)  16.6 us
  transfers between devices with their start and end apart: 7, of which 4 were waited for; matrix products, arithmetic and copies ran while one was open for 9% of the time, Pallas kernels for 0%

commit v1 on v0

v1 whole, which is shorter than its diff:
```python
import jax
import jax.numpy as jnp
from jax import lax
from jax.experimental import pallas as pl
from jax.experimental.pallas import tpu as pltpu
from jax.sharding import PartitionSpec as P

MESH = pl.DeviceIdType.MESH
ROWS = 16
COLS = 8
SLOTS = 10
BS = 128
CUT = BS // ROWS
OTHERS = 2
WANT = SLOTS * OTHERS


def halves(x):
    high = x.astype(jnp.bfloat16)
    low = (x - high.astype(jnp.float32)).astype(jnp.bfloat16)
    return high, low


def left_operand(blocks):
    pairs = [halves(block) for block in blocks]
    parts = [half for pair in pairs for half in pair] + [high for high, _ in pairs]
    return jnp.concatenate(parts, axis=1)


def right_operand(blocks):
    pairs = [halves(block) for block in blocks]
    parts = [high for high, _ in pairs for _ in range(2)] + [low for _, low in pairs]
    return jnp.concatenate(parts, axis=0)


def product(left, right):
    return jnp.dot(left, right, preferred_element_type=jnp.float32)


def kernel(
    d_ref, h_ref, rows_ref, cols_ref, left_ref, right_ref,
    new_ref, ew_ref,
    pan_d, pan_q, own_h, deal_d, deal_h, deal_q, stage, got, mix_base, mix_dir, want_v, want_s, part, part_row, part_col,
    local_sem, near_send, near_recv, deal_send, deal_recv, got_send, got_recv,
    want_send, want_recv, row_send, row_recv, col_send, col_recv,
):
    r, c = lax.axis_index("row"), lax.axis_index("col")
    up, down = lax.rem(c + 1, COLS), lax.rem(c + COLS - 1, COLS)
    first = r * SLOTS
    deal = (deal_d, deal_h, deal_q)
    own_d, own_q = pan_d.at[pl.ds(SLOTS, SLOTS)], pan_q.at[pl.ds(SLOTS, SLOTS)]

    load_d = pltpu.make_async_copy(d_ref, own_d, local_sem.at[0])
    load_h = pltpu.make_async_copy(h_ref, own_h, local_sem.at[1])
    load_d.start()
    load_h.start()

    def row_peer(step):
        return lax.rem(r + step, ROWS)

    def col_peer(step):
        return lax.rem(c + step, COLS)

    barrier = pltpu.get_barrier_semaphore()

    @pl.loop(1, ROWS)
    def _(step):
        pl.semaphore_signal(barrier, inc=1, device_id=(row_peer(step), c), device_id_type=MESH)

    @pl.loop(1, COLS)
    def _(step):
        pl.semaphore_signal(barrier, inc=1, device_id=(r, col_peer(step)), device_id_type=MESH)

    lane = lax.broadcasted_iota(jnp.int32, (1, BS), 1)
    wanted = jnp.zeros((1, BS), jnp.int32)
    for s in range(SLOTS):
        own = first + s
        one, two, three = right_ref[s, 0], right_ref[s, 1], right_ref[s, 2]
        u0 = jnp.maximum(jnp.where(one == own, two, one), 0)
        u1 = jnp.maximum(jnp.where(three == own, two, three), 0)
        wanted = jnp.where(lane == 2 * s, u0, jnp.where(lane == 2 * s + 1, u1, wanted))
    want_v[r] = wanted

    zero_block = jnp.zeros((BS, BS), jnp.float32)
    pan_d[3 * SLOTS] = zero_block
    pan_q[3 * SLOTS] = zero_block

    pl.semaphore_wait(barrier, ROWS + COLS - 2)

    def want_copy(src, dst, peer):
        return pltpu.make_async_remote_copy(
            src_ref=want_v.at[src], dst_ref=want_v.at[src], send_sem=want_send.at[dst], recv_sem=want_recv.at[src],
            device_id=(peer, c), device_id_type=MESH,
        )

    def deal_copy(k, own, src, dst, peer):
        return pltpu.make_async_remote_copy(
            src_ref=own.at[:, pl.ds(pl.multiple_of(dst * CUT, CUT), CUT), :],
            dst_ref=deal[k].at[pl.ds(src * SLOTS, SLOTS)],
            send_sem=deal_send.at[k, dst], recv_sem=deal_recv.at[k, src],
            device_id=(peer, c), device_id_type=MESH,
        )

    def got_copy(k, src, dst, peer):
        return pltpu.make_async_remote_copy(
            src_ref=stage.at[k, dst], dst_ref=got.at[k, src],
            send_sem=got_send.at[k, dst], recv_sem=got_recv.at[k, src],
            device_id=(peer, c), device_id_type=MESH,
        )

    def near_copies(k, own, pan):
        to_up = pltpu.make_async_remote_copy(
            src_ref=own, dst_ref=pan.at[pl.ds(0, SLOTS)],
            send_sem=near_send.at[k, 0], recv_sem=near_recv.at[k, 0],
            device_id=(r, up), device_id_type=MESH,
        )
        to_down = pltpu.make_async_remote_copy(
            src_ref=own, dst_ref=pan.at[pl.ds(2 * SLOTS, SLOTS)],
            send_sem=near_send.at[k, 1], recv_sem=near_recv.at[k, 1],
            device_id=(r, down), device_id_type=MESH,
        )
        return to_up, to_down

    def deal_out(k, own):
        @pl.loop(1, ROWS)
        def _(step):
            dst = row_peer(step)
            deal_copy(k, own, r, dst, dst).start()

        mine = pl.ds(pl.multiple_of(r * CUT, CUT), CUT)
        for s in range(SLOTS):
            deal[k][first + s] = own[s, mine, :]

    def deal_in(k, own):
        @pl.loop(1, ROWS)
        def _(step):
            src = row_peer(step)
            deal_copy(k, own, src, r, src).wait_recv()

    def pass_on(k):
        @pl.loop(1, ROWS)
        def _(step):
            dst = row_peer(step)
            for q in range(WANT):
                stage[k, dst, q] = deal[k][want_s[dst, 0, q]]
            got_copy(k, r, dst, dst).start()

        for q in range(WANT):
            got[k, r, q] = deal[k][want_s[r, 0, q]]

    def get_in(k):
        @pl.loop(1, ROWS)
        def _(step):
            src = row_peer(step)
            got_copy(k, src, r, src).wait_recv()

    def fetched(k, place):
        return got[k, :, place].reshape(BS, BS)

    def left_blocks(pan, s):
        own = first + s
        places = []
        for t in range(3):
            index = left_ref[s, t]
            held = jnp.maximum(index, 0)
            owner = lax.div(held, SLOTS)
            within = held - owner * SLOTS
            near = lax.rem(owner - c + 1 + COLS, COLS)
            places.append(jnp.where(index >= 0, jnp.minimum(near * SLOTS + within, 3 * SLOTS), 3 * SLOTS))
        first_is, second_is, third_is = (right_ref[s, t] == own for t in range(3))
        self_place = jnp.where(first_is, places[0], jnp.where(second_is, places[1], places[2]))
        u0 = jnp.where(first_is, places[1], places[0])
        u1 = jnp.where(third_is, places[1], places[2])
        return [pan[self_place], pan[u0], pan[u1]]

    load_d.wait()
    near_d = near_copies(0, own_d, pan_d)

    @pl.loop(1, ROWS)
    def _(step):
        dst = row_peer(step)
        want_copy(r, dst, dst).start()

    deal_out(0, own_d)
    for copy in near_d:
        copy.start()
    load_h.wait()
    deal_out(1, own_h)

    @pl.loop(1, ROWS)
    def _(step):
        src = row_peer(step)
        want_copy(src, r, src).wait_recv()

    to_smem = pltpu.make_async_copy(want_v, want_s, local_sem.at[2])
    to_smem.start()
    to_smem.wait()

    deal_in(0, own_d)
    pass_on(0)
    deal_in(1, own_h)
    pass_on(1)
    for copy in near_d:
        copy.wait_recv()
    get_in(0)

    eye = lax.broadcasted_iota(jnp.int32, (BS, BS), 0) == lax.broadcasted_iota(jnp.int32, (BS, BS), 1)

    def trace_row(block, s):
        on = (rows_ref[0, s] == cols_ref[0, s]).astype(jnp.float32)
        return jnp.sum(jnp.where(eye, block, 0.0), axis=0, keepdims=True) * on

    part[...] = jnp.zeros_like(part)

    @pl.loop(0, SLOTS)
    def _(s):
        own = pan_d[SLOTS + s]
        right = right_operand([own, fetched(0, 2 * s), fetched(0, 2 * s + 1)])
        square = product(left_operand(left_blocks(pan_d, s)), right)
        pan_q[SLOTS + s] = square
        part[0:1, :] += trace_row(own, s)
        part[1:2, :] += trace_row(square, s)

    near_q = near_copies(1, own_q, pan_q)
    deal_out(2, own_q)
    for copy in near_q:
        copy.start()
    deal_in(2, own_q)
    pass_on(2)
    for copy in near_q:
        copy.wait_recv()
    get_in(2)

    @pl.loop(0, SLOTS)
    def _(s):
        left = left_operand(left_blocks(pan_q, s))
        square = pan_q[SLOTS + s]
        right_d = right_operand([pan_d[SLOTS + s], fetched(0, 2 * s), fetched(0, 2 * s + 1)])
        right_q = right_operand([square, fetched(2, 2 * s), fetched(2, 2 * s + 1)])
        both = product(left, jnp.concatenate([right_d, right_q], axis=1))
        cube, fourth = both[:, :BS], both[:, BS:]
        mix_base[s] = 4.0 * cube - 3.0 * fourth
        mix_dir[s] = fourth - 2.0 * cube + square
        part[2:3, :] += trace_row(cube, s)
        part[3:4, :] += trace_row(fourth, s)

    def row_copy(src, dst, peer):
        return pltpu.make_async_remote_copy(
            src_ref=part, dst_ref=part_row.at[src], send_sem=row_send.at[dst], recv_sem=row_recv.at[src],
            device_id=(peer, c), device_id_type=MESH,
        )

    def col_copy(src, dst, peer):
        return pltpu.make_async_remote_copy(
            src_ref=part_col.at[src], dst_ref=part_col.at[src], send_sem=col_send.at[dst], recv_sem=col_recv.at[src],
            device_id=(r, peer), device_id_type=MESH,
        )

    @pl.loop(1, ROWS)
    def _(step):
        dst = row_peer(step)
        row_copy(r, dst, dst).start()

    part_row[r] = part[...]
    get_in(1)

    @pl.loop(0, SLOTS)
    def _(s):
        right = right_operand([own_h[s], fetched(1, 2 * s), fetched(1, 2 * s + 1)])
        ew_ref[s] = product(left_operand(left_blocks(pan_q, s)), right)

    @pl.loop(1, ROWS)
    def _(step):
        src = row_peer(step)
        row_copy(src, r, src).wait_recv()

    part_col[c] = jnp.sum(part_row[...], axis=0)

    @pl.loop(1, COLS)
    def _(step):
        dst = col_peer(step)
        col_copy(c, dst, dst).start()

    @pl.loop(1, COLS)
    def _(step):
        src = col_peer(step)
        col_copy(src, c, src).wait_recv()

    traces = jnp.sum(jnp.sum(part_col[...], axis=0), axis=1, keepdims=True)
    one, two, three, four = (traces[k : k + 1, :] for k in range(4))
    trace_f = 4.0 * three - 3.0 * four
    trace_g = four - 2.0 * three + two
    gamma = jnp.clip((one - trace_f) / jnp.maximum(jnp.abs(trace_g), 1.0), 0.0, 6.0)

    @pl.loop(0, SLOTS)
    def _(s):
        new_ref[s] = mix_base[s] + gamma * mix_dir[s]

    for copy in (*near_d, *near_q):
        copy.wait_send()

    @pl.loop(1, ROWS)
    def _(step):
        dst = row_peer(step)
        want_copy(r, dst, dst).wait_send()
        row_copy(r, dst, dst).wait_send()
        for k, own in enumerate((own_d, own_h, own_q)):
            deal_copy(k, own, r, dst, dst).wait_send()
            got_copy(k, r, dst, dst).wait_send()

    @pl.loop(1, COLS)
    def _(step):
        dst = col_peer(step)
        col_copy(c, dst, dst).wait_send()


def shards(density, hamiltonian, block_rows, block_cols, left_index, right_index):
    any_space = pl.BlockSpec(memory_space=pl.ANY)
    smem = pl.BlockSpec(memory_space=pltpu.SMEM)
    vmem = pl.BlockSpec(memory_space=pltpu.VMEM)
    block = jax.ShapeDtypeStruct((SLOTS, BS, BS), jnp.float32)
    dma = pltpu.SemaphoreType.DMA
    new, ew = pl.pallas_call(
        kernel,
        out_shape=(block, block),
        in_specs=[any_space, any_space, smem, smem, smem, smem],
        out_specs=(vmem, vmem),
        scratch_shapes=[
            pltpu.VMEM((3 * SLOTS + 1, BS, BS), jnp.float32),
            pltpu.VMEM((3 * SLOTS + 1, BS, BS), jnp.float32),
            pltpu.VMEM((SLOTS, BS, BS), jnp.float32),
            pltpu.VMEM((ROWS * SLOTS, CUT, BS), jnp.float32),
            pltpu.VMEM((ROWS * SLOTS, CUT, BS), jnp.float32),
            pltpu.VMEM((ROWS * SLOTS, CUT, BS), jnp.float32),
            pltpu.VMEM((3, ROWS, WANT, CUT, BS), jnp.float32),
            pltpu.VMEM((3, ROWS, WANT, CUT, BS), jnp.float32),
            pltpu.VMEM((SLOTS, BS, BS), jnp.float32),
            pltpu.VMEM((SLOTS, BS, BS), jnp.float32),
            pltpu.VMEM((ROWS, 1, BS), jnp.int32),
            pltpu.SMEM((ROWS, 1, BS), jnp.int32),
            pltpu.VMEM((8, BS), jnp.float32),
            pltpu.VMEM((ROWS, 8, BS), jnp.float32),
            pltpu.VMEM((COLS, 8, BS), jnp.float32),
            dma((3,)),
            dma((2, 2)),
            dma((2, 2)),
            dma((3, ROWS)),
            dma((3, ROWS)),
            dma((3, ROWS)),
            dma((3, ROWS)),
            dma((ROWS,)),
            dma((ROWS,)),
            dma((ROWS,)),
            dma((ROWS,)),
            dma((COLS,)),
            dma((COLS,)),
        ],
        compiler_params=pltpu.CompilerParams(
            collective_id=0, has_side_effects=True, vmem_limit_bytes=40 * 1024 * 1024
        ),
        cost_estimate=pl.CostEstimate(flops=2 * 9 * 4 * SLOTS * BS**3, bytes_accessed=5 * SLOTS * BS * BS, transcendentals=0),
    )(density[0], hamiltonian[0], block_rows, block_cols, left_index[0], right_index[0])
    return new[None], ew[None]


def solution(mesh):
    in_specs = (
        P("row", "col", None, None),
        P("row", "col", None, None),
        P("row", "col"),
        P("row", "col"),
        P("row", "col", None),
        P("row", "col", None),
    )
    out_specs = (P("row", "col", None, None), P("row", "col", None, None))
    return jax.shard_map(shards, mesh=mesh, in_specs=in_specs, out_specs=out_specs, check_vma=False)
```

time: 351 us -> 106 us (0.30)
  waiting for transfers between devices: 216 us -> 0 us
  Pallas kernels: 0 us -> 99.2 us
  blocking collectives: 64.9 us -> 0 us
  matrix products: 17.1 us -> 0 us
  between operations: 17.6 us -> 0.65 us
  local copies, waits for them, and re-layouts: 21.4 us -> 6.06 us
  other arithmetic: 8.27 us -> 0 us
  starting transfers between devices: 4.64 us -> 0 us
    all_gather x3 -> x0, waiting for transfers between devices: 210 us -> none  [the longest x1 70.5 us: shards(): lax.all_gather(density, 'row', axis=0, tiled=True)]
    pallas_call x0 -> x1, Pallas kernels: none -> 99.2 us  [shards(): pl.pallas_call(kernel, out_shape=(block, block), in_specs=[any_space, any...]
    psum x1 -> x0, blocking collectives: 64.9 us -> none  [shards(): trace_one, trace_two = lax.psum((trace_one, trace_two), ('row', 'col'))]
    gather x5 -> x0, local copies, waits for them, and re-layouts: 20.7 us -> none  [the longest x3 16.6 us: stack_product(): right_blocks = jnp.take(col_panel, jnp.maximum(right_part, 0), axis=0)]
    dot_general x4 -> x0, matrix products: 17.1 us -> none  [stack_product(): jnp.einsum('stij,stjk->sik', left_blocks, right_blocks, precision=lax.Pre...]
    unnamed x12 -> x14, local copies, waits for them, and re-layouts: 0.03 us -> 5.87 us
    ppermute x4 -> x0, waiting for transfers between devices: 5.23 us -> none  [the longest x2 5.23 us: extended(): after = lax.ppermute(leading, axis, down)]
    ppermute x4 -> x0, starting transfers between devices: 4.53 us -> none  [the longest x2 2.41 us: extended(): before = lax.ppermute(last, axis, up)]
  transfers between devices with their start and end apart: 7 -> 0, of which waited for: 4 -> 0; matrix products, arithmetic and copies ran while one was open for 9% -> 0% of each run, Pallas kernels for 0% -> 0%
where the time goes in v1:
time: 106 us
  Pallas kernels  99.2 us (94%)
  local copies, waits for them, and re-layouts  6.06 us (6%)
    pallas_call x1, Pallas kernels, shards(): pl.pallas_call(kernel, out_shape=(block, block), in_specs=[any_space, any...  99.2 us
    unnamed x14, local copies, waits for them, and re-layouts  5.87 us

profile of v1, /device:TPU:1, one launch (start us, length us, event | category | flops | bytes accessed | tf_op | source)
XLA Modules:
  0.0 105.9 jit_solution(1982555396682835519)
XLA Ops:
  0.6 0.0 copy-start.4
  0.6 0.7 copy-done.4
  1.3 0.1 copy.10
  1.4 0.0 copy-start.5
  1.4 0.7 copy-done.5
  2.1 0.1 copy.11
  2.2 0.0 copy-start.2
  2.2 0.0 copy-start.3
  2.2 0.7 copy-done.2
  2.8 0.0 copy-done.3
  2.9 0.0 copy-start
  2.9 1.1 %copy-done = f32[1,10,128,128]{3,2,1,0:T(8,128)S(1)} copy-done((f32[1,10,128,128]{3,2,1,0:T(8,128)S(1)}, f32[1,10,128,128]{3,2,1,0:T(8,128)}, u32[]{:S(2)}) %copy-start) | copy-done | bytes 655384
  3.9 0.0 copy-start.1
  3.9 1.1 %copy-done.1 = f32[1,10,128,128]{3,2,1,0:T(8,128)S(1)} copy-done((f32[1,10,128,128]{3,2,1,0:T(8,128)S(1)}, f32[1,10,128,128]{3,2,1,0:T(8,128)}, u32[]{:S(2)}) %copy-start.1) | copy-done | bytes 655384
  5.0 99.2 %shard_map.77 = (f32[10,128,128]{2,1,0:T(8,128)S(1)}, f32[10,128,128]{2,1,0:T(8,128)S(1)}) custom-call(f32[10,128,128]{2,1,0:T(8,128)S(1)} %bitcast.10, f32[10,128,128]{2,1,0:T(8,128)S(1)} %bitcast.11, s32[1,10]{1,0:T(1,128)S(1)} %copy-done.2, s32[1,10]{1,0:T(1,128)S(1)} %copy-done.3, s32[10,3]{1,0:T(8,128)S(1)} %bitcast.8, s32[10,3]{1,0:T(8,128)S(1)} %bitcast.9), custom_call_target="tpu_custom_call" | custom-call | flops 1509949440 | bytes 819200 | tf_op jit(solution)/shard_map/pallas_call | solution.py:323
  104.2 0.8 copy.14
  105.1 0.8 copy.15
Async XLA Ops:
  0.6 0.7 copy-start.4
  1.4 0.7 copy-start.5
  2.2 0.7 copy-start.2
  2.2 0.7 copy-start.3
  2.9 1.1 %copy-start = (f32[1,10,128,128]{3,2,1,0:T(8,128)S(1)}, f32[1,10,128,128]{3,2,1,0:T(8,128)}, u32[]{:S(2)}) copy-start(f32[1,10,128,128]{3,2,1,0:T(8,128)} %param.6) | copy-start | bytes 1966084
  3.9 1.1 %copy-start.1 = (f32[1,10,128,128]{3,2,1,0:T(8,128)S(1)}, f32[1,10,128,128]{3,2,1,0:T(8,128)}, u32[]{:S(2)}) copy-start(f32[1,10,128,128]{3,2,1,0:T(8,128)} %param.7) | copy-start | bytes 1966084

commit v2 on v1

v2 whole, which is shorter than its diff:
```python
import functools

import jax
import jax.numpy as jnp
from jax import lax
from jax.experimental import pallas as pl
from jax.experimental.pallas import tpu as pltpu
from jax.sharding import PartitionSpec as P

MESH = pl.DeviceIdType.MESH
ROWS = 16
COLS = 8
SLOTS = 10
BS = 128
CUT = BS // ROWS
OTHERS = 2
WANT_MOST = SLOTS * OTHERS
WANT_FEW = 8


def halves(x):
    high = x.astype(jnp.bfloat16)
    low = (x - high.astype(jnp.float32)).astype(jnp.bfloat16)
    return high, low


def left_operand(blocks):
    pairs = [halves(block) for block in blocks]
    parts = [half for pair in pairs for half in pair] + [high for high, _ in pairs]
    return jnp.concatenate(parts, axis=1)


def right_operand(blocks):
    pairs = [halves(block) for block in blocks]
    parts = [high for high, _ in pairs for _ in range(2)] + [low for _, low in pairs]
    return jnp.concatenate(parts, axis=0)


def product(left, right):
    return jnp.dot(left, right, preferred_element_type=jnp.float32)


def kernel(
    cap,
    d_ref, h_ref, rows_ref, cols_ref, left_ref, right_ref,
    new_ref, ew_ref, over_ref,
    pan_d, pan_q, own_h, deal_d, deal_h, deal_q, stage, got_d, got_h, got_q, mix_base, mix_dir, new_v, ew_v,
    rows_s, cols_s, left_s, right_s, place_s, want_v, want_s, part, part_row, part_col,
    local_sem, near_send, near_recv, deal_send, deal_recv, got_send, got_recv,
    want_send, want_recv, row_send, row_recv, col_send, col_recv,
):
    r, c = lax.axis_index("row"), lax.axis_index("col")
    up, down = lax.rem(c + 1, COLS), lax.rem(c + COLS - 1, COLS)
    first = r * SLOTS
    deal, got = (deal_d, deal_h, deal_q), (got_d, got_h, got_q)
    own_d, own_q = pan_d.at[pl.ds(SLOTS, SLOTS)], pan_q.at[pl.ds(SLOTS, SLOTS)]

    def row_peer(step):
        return lax.rem(r + step, ROWS)

    def col_peer(step):
        return lax.rem(c + step, COLS)

    barrier = pltpu.get_barrier_semaphore()

    @pl.loop(1, ROWS)
    def _(step):
        pl.semaphore_signal(barrier, inc=1, device_id=(row_peer(step), c), device_id_type=MESH)

    @pl.loop(1, COLS)
    def _(step):
        pl.semaphore_signal(barrier, inc=1, device_id=(r, col_peer(step)), device_id_type=MESH)

    loads = [
        pltpu.make_async_copy(src, dst, local_sem.at[k])
        for k, (src, dst) in enumerate(
            (
                (right_ref, right_s),
                (d_ref, own_d),
                (left_ref, left_s),
                (h_ref, own_h),
                (rows_ref, rows_s),
                (cols_ref, cols_s),
            )
        )
    ]
    for load in loads:
        load.start()
    loads[0].wait()

    lane = lax.broadcasted_iota(jnp.int32, (1, BS), 1)
    wanted = jnp.zeros((1, BS), jnp.int32)
    count = jnp.int32(0)
    for s in range(SLOTS):
        own = first + s
        one, two, three = (right_s[t, 0, s] for t in range(3))
        for u, index in enumerate((jnp.where(one == own, two, one), jnp.where(three == own, two, three))):
            live = index >= 0
            near = index - first
            here = jnp.logical_and(near >= 0, near < SLOTS)
            away = jnp.logical_and(live, jnp.logical_not(here))
            place_s[2 * s + u] = jnp.where(away, jnp.minimum(count, cap - 1), jnp.where(here, cap + near, 0))
            wanted = jnp.where(lane == jnp.where(away, count, -1), index, wanted)
            count = count + away.astype(jnp.int32)
    want_v[r] = wanted
    over = jnp.where(count > cap, 1.0, 0.0)

    zero_block = jnp.zeros((BS, BS), jnp.float32)
    pan_d[3 * SLOTS] = zero_block
    pan_q[3 * SLOTS] = zero_block
    loads[1].wait()

    pl.semaphore_wait(barrier, ROWS + COLS - 2)

    def want_copy(src, dst, peer):
        return pltpu.make_async_remote_copy(
            src_ref=want_v.at[src], dst_ref=want_v.at[src], send_sem=want_send.at[dst], recv_sem=want_recv.at[src],
            device_id=(peer, c), device_id_type=MESH,
        )

    def deal_copy(k, own, src, dst, peer):
        return pltpu.make_async_remote_copy(
            src_ref=own.at[:, pl.ds(pl.multiple_of(dst * CUT, CUT), CUT), :],
            dst_ref=deal[k].at[pl.ds(src * SLOTS, SLOTS)],
            send_sem=deal_send.at[k, dst], recv_sem=deal_recv.at[k, src],
            device_id=(peer, c), device_id_type=MESH,
        )

    def got_copy(k, src, dst, peer):
        return pltpu.make_async_remote_copy(
            src_ref=stage.at[k, dst], dst_ref=got[k].at[src, pl.ds(0, cap)],
            send_sem=got_send.at[k, dst], recv_sem=got_recv.at[k, src],
            device_id=(peer, c), device_id_type=MESH,
        )

    def near_copies(k, own, pan):
        to_up = pltpu.make_async_remote_copy(
            src_ref=own, dst_ref=pan.at[pl.ds(0, SLOTS)],
            send_sem=near_send.at[k, 0], recv_sem=near_recv.at[k, 0],
            device_id=(r, up), device_id_type=MESH,
        )
        to_down = pltpu.make_async_remote_copy(
            src_ref=own, dst_ref=pan.at[pl.ds(2 * SLOTS, SLOTS)],
            send_sem=near_send.at[k, 1], recv_sem=near_recv.at[k, 1],
            device_id=(r, down), device_id_type=MESH,
        )
        return to_up, to_down

    def deal_out(k, own):
        @pl.loop(1, ROWS)
        def _(step):
            dst = row_peer(step)
            deal_copy(k, own, r, dst, dst).start()

        mine = pl.ds(pl.multiple_of(r * CUT, CUT), CUT)
        for s in range(SLOTS):
            deal[k][first + s] = own[s, mine, :]
            got[k][:, cap + s] = own[s].reshape(ROWS, CUT, BS)

    def deal_in(k, own):
        @pl.loop(1, ROWS)
        def _(step):
            src = row_peer(step)
            deal_copy(k, own, src, r, src).wait_recv()

    def pick(k, dst, q):
        return deal[k][want_s[dst, 0, q]]

    def pass_on(k):
        @pl.loop(1, ROWS)
        def _(step):
            dst = row_peer(step)
            for q in range(cap):
                stage[k, dst, q] = pick(k, dst, q)
            got_copy(k, r, dst, dst).start()

        for q in range(cap):
            got[k][r, q] = pick(k, r, q)

    def get_in(k):
        @pl.loop(1, ROWS)
        def _(step):
            src = row_peer(step)
            got_copy(k, src, r, src).wait_recv()

    def right_blocks(k, s):
        places = (cap + s, place_s[2 * s], place_s[2 * s + 1])
        return right_operand([got[k][:, place].reshape(BS, BS) for place in places])

    def left_blocks(pan, s):
        own = first + s
        places = []
        for t in range(3):
            index = left_s[t, 0, s]
            held = jnp.maximum(index, 0)
            owner = lax.div(held, SLOTS)
            within = held - owner * SLOTS
            near = lax.rem(owner - c + 1 + COLS, COLS)
            place = jnp.minimum(near * SLOTS + within, 3 * SLOTS)
            places.append(jnp.where(index >= 0, place, 3 * SLOTS))
        first_is, second_is, third_is = (right_s[t, 0, s] == own for t in range(3))
        self_place = jnp.where(first_is, places[0], jnp.where(second_is, places[1], places[2]))
        u0 = jnp.where(first_is, places[1], places[0])
        u1 = jnp.where(third_is, places[1], places[2])
        return left_operand([pan[self_place], pan[u0], pan[u1]])

    @pl.loop(1, ROWS)
    def _(step):
        dst = row_peer(step)
        want_copy(r, dst, dst).start()

    near_d = near_copies(0, own_d, pan_d)
    deal_out(0, own_d)
    for copy in near_d:
        copy.start()

    @pl.loop(1, ROWS)
    def _(step):
        src = row_peer(step)
        want_copy(src, r, src).wait_recv()

    to_smem = pltpu.make_async_copy(want_v, want_s, local_sem.at[6])
    to_smem.start()
    for load in loads[2:]:
        load.wait()
    to_smem.wait()

    deal_in(0, own_d)
    pass_on(0)
    deal_out(1, own_h)
    for copy in near_d:
        copy.wait_recv()
    get_in(0)

    eye = lax.broadcasted_iota(jnp.int32, (BS, BS), 0) == lax.broadcasted_iota(jnp.int32, (BS, BS), 1)

    def trace_row(block, s):
        on = (rows_s[0, s] == cols_s[0, s]).astype(jnp.float32)
        return jnp.sum(jnp.where(eye, block, 0.0), axis=0, keepdims=True) * on

    part[...] = jnp.zeros_like(part)

    @pl.loop(0, SLOTS)
    def _(s):
        square = product(left_blocks(pan_d, s), right_blocks(0, s))
        pan_q[SLOTS + s] = square
        part[0:1, :] += trace_row(pan_d[SLOTS + s], s)
        part[1:2, :] += trace_row(square, s)

    near_q = near_copies(1, own_q, pan_q)
    deal_out(2, own_q)
    for copy in near_q:
        copy.start()
    deal_in(1, own_h)
    deal_in(2, own_q)
    pass_on(2)
    pass_on(1)
    for copy in near_q:
        copy.wait_recv()
    get_in(2)

    @pl.loop(0, SLOTS)
    def _(s):
        square = pan_q[SLOTS + s]
        both = product(left_blocks(pan_q, s), jnp.concatenate([right_blocks(0, s), right_blocks(2, s)], axis=1))
        cube, fourth = both[:, :BS], both[:, BS:]
        mix_base[s] = 4.0 * cube - 3.0 * fourth
        mix_dir[s] = fourth - 2.0 * cube + square
        part[2:3, :] += trace_row(cube, s)
        part[3:4, :] += trace_row(fourth, s)

    part[4:5, :] = jnp.zeros((1, BS), jnp.float32) + over

    def row_copy(src, dst, peer):
        return pltpu.make_async_remote_copy(
            src_ref=part, dst_ref=part_row.at[src], send_sem=row_send.at[dst], recv_sem=row_recv.at[src],
            device_id=(peer, c), device_id_type=MESH,
        )

    def col_copy(src, dst, peer):
        return pltpu.make_async_remote_copy(
            src_ref=part_col.at[src], dst_ref=part_col.at[src], send_sem=col_send.at[dst], recv_sem=col_recv.at[src],
            device_id=(r, peer), device_id_type=MESH,
        )

    @pl.loop(1, ROWS)
    def _(step):
        dst = row_peer(step)
        row_copy(r, dst, dst).start()

    part_row[r] = part[...]

    @pl.loop(1, ROWS)
    def _(step):
        src = row_peer(step)
        row_copy(src, r, src).wait_recv()

    part_col[c] = jnp.sum(part_row[...], axis=0)

    @pl.loop(1, COLS)
    def _(step):
        dst = col_peer(step)
        col_copy(c, dst, dst).start()

    get_in(1)

    @pl.loop(0, SLOTS)
    def _(s):
        ew_v[s] = product(left_blocks(pan_q, s), right_blocks(1, s))

    put_ew = pltpu.make_async_copy(ew_v, ew_ref, local_sem.at[7])
    put_ew.start()

    @pl.loop(1, COLS)
    def _(step):
        src = col_peer(step)
        col_copy(src, c, src).wait_recv()

    sums = jnp.sum(part_col[...], axis=0)
    over_ref[0, 0] = jnp.sum(sums[4:5, :])
    traces = jnp.sum(sums, axis=1, keepdims=True)
    one, two, three, four = (traces[k : k + 1, :] for k in range(4))
    trace_f = 4.0 * three - 3.0 * four
    trace_g = four - 2.0 * three + two
    gamma = jnp.clip((one - trace_f) / jnp.maximum(jnp.abs(trace_g), 1.0), 0.0, 6.0)

    @pl.loop(0, SLOTS)
    def _(s):
        new_v[s] = mix_base[s] + gamma * mix_dir[s]

    put_new = pltpu.make_async_copy(new_v, new_ref, local_sem.at[8])
    put_new.start()

    for copy in (*near_d, *near_q):
        copy.wait_send()

    @pl.loop(1, ROWS)
    def _(step):
        dst = row_peer(step)
        want_copy(r, dst, dst).wait_send()
        row_copy(r, dst, dst).wait_send()
        for k, own in enumerate((own_d, own_h, own_q)):
            deal_copy(k, own, r, dst, dst).wait_send()
            got_copy(k, r, dst, dst).wait_send()

    @pl.loop(1, COLS)
    def _(step):
        dst = col_peer(step)
        col_copy(c, dst, dst).wait_send()

    put_ew.wait()
    put_new.wait()


def step(cap, collective_id, *operands):
    any_space = pl.BlockSpec(memory_space=pl.ANY)
    smem = pl.BlockSpec(memory_space=pltpu.SMEM)
    block = jax.ShapeDtypeStruct((SLOTS, BS, BS), jnp.float32)
    dma = pltpu.SemaphoreType.DMA
    panel = pltpu.VMEM((3 * SLOTS + 1, BS, BS), jnp.float32)
    own = pltpu.VMEM((SLOTS, BS, BS), jnp.float32)
    dealt = pltpu.VMEM((ROWS * SLOTS, CUT, BS), jnp.float32)
    fetched = pltpu.VMEM((ROWS, cap + SLOTS, CUT, BS), jnp.float32)
    return pl.pallas_call(
        functools.partial(kernel, cap),
        out_shape=(block, block, jax.ShapeDtypeStruct((1, 1), jnp.float32)),
        in_specs=[any_space] * 6,
        out_specs=(any_space, any_space, smem),
        scratch_shapes=[
            panel,
            panel,
            own,
            dealt,
            dealt,
            dealt,
            pltpu.VMEM((3, ROWS, cap, CUT, BS), jnp.float32),
            fetched,
            fetched,
            fetched,
            own,
            own,
            own,
            own,
            pltpu.SMEM((1, SLOTS), jnp.int32),
            pltpu.SMEM((1, SLOTS), jnp.int32),
            pltpu.SMEM((3, 1, SLOTS), jnp.int32),
            pltpu.SMEM((3, 1, SLOTS), jnp.int32),
            pltpu.SMEM((WANT_MOST,), jnp.int32),
            pltpu.VMEM((ROWS, 1, BS), jnp.int32),
            pltpu.SMEM((ROWS, 1, BS), jnp.int32),
            pltpu.VMEM((8, BS), jnp.float32),
            pltpu.VMEM((ROWS, 8, BS), jnp.float32),
            pltpu.VMEM((COLS, 8, BS), jnp.float32),
            dma((9,)),
            dma((2, 2)),
            dma((2, 2)),
            dma((3, ROWS)),
            dma((3, ROWS)),
            dma((3, ROWS)),
            dma((3, ROWS)),
            dma((ROWS,)),
            dma((ROWS,)),
            dma((ROWS,)),
            dma((ROWS,)),
            dma((COLS,)),
            dma((COLS,)),
        ],
        compiler_params=pltpu.CompilerParams(
            collective_id=collective_id, has_side_effects=True, vmem_limit_bytes=60 * 1024 * 1024
        ),
        cost_estimate=pl.CostEstimate(flops=2 * 9 * 4 * SLOTS * BS**3, bytes_accessed=5 * SLOTS * BS * BS, transcendentals=0),
    )(*operands)


def shards(density, hamiltonian, block_rows, block_cols, left_index, right_index):
    terms_first = (2, 0, 1)
    operands = (
        density[0], hamiltonian[0], block_rows, block_cols,
        jnp.transpose(left_index, terms_first), jnp.transpose(right_index, terms_first),
    )
    new, ew, over = step(WANT_FEW, 0, *operands)
    new, ew = lax.cond(
        over[0, 0] > 0.0,
        lambda new, ew, *operands: tuple(step(WANT_MOST, 1, *operands)[:2]),
        lambda new, ew, *operands: (new, ew),
        new, ew, *operands,
    )
    return new[None], ew[None]


def solution(mesh):
    in_specs = (
        P("row", "col", None, None),
        P("row", "col", None, None),
        P("row", "col"),
        P("row", "col"),
        P("row", "col", None),
        P("row", "col", None),
    )
    out_specs = (P("row", "col", None, None), P("row", "col", None, None))
    return jax.shard_map(shards, mesh=mesh, in_specs=in_specs, out_specs=out_specs, check_vma=False)
```

time: 106 us -> 70.4 us (0.66)
  Pallas kernels: 99.2 us -> 66.5 us
  local copies, waits for them, and re-layouts: 6.06 us -> 2.36 us
    pallas_call x1, Pallas kernels: 99.2 us -> 66.5 us  [step(): pl.pallas_call(functools.partial(kernel, cap), out_shape=(block, block, j...]
    unnamed x14, local copies, waits for them, and re-layouts: 5.87 us -> 2.36 us
where the time goes in v2:
time: 70.4 us; the launch traced here: 70.2 us
  Pallas kernels  66.5 us (94%)
  local copies, waits for them, and re-layouts  2.36 us (3%)
  between operations  1.33 us (2%)
    pallas_call x1, Pallas kernels, step(): pl.pallas_call(functools.partial(kernel, cap), out_shape=(block, block, j...  66.5 us
    unnamed x14, local copies, waits for them, and re-layouts  2.36 us

profile of v2, /device:TPU:1, one launch (start us, length us, event | category | flops | bytes accessed | tf_op | source)
XLA Modules:
  0.0 70.2 jit_solution(6354433050954774747)
XLA Ops:
  0.6 0.0 copy-start.5
  0.6 0.0 copy-start.2
  0.7 0.0 copy-start.3
  0.7 0.0 copy-start.4
  0.7 0.6 copy-done.5
  1.3 0.0 copy-done.2
  1.3 0.0 copy-done.3
  1.3 0.0 copy-done.4
  1.3 0.0 copy-start
  1.3 0.0 copy-start.1
  1.4 66.5 %shard_map.77 = (f32[10,128,128]{2,1,0:T(8,128)S(1)}, f32[10,128,128]{2,1,0:T(8,128)S(1)}, f32[1,1]{1,0:T(1,128)}) custom-call(f32[10,128,128]{2,1,0:T(8,128)} %bitcast.13, f32[10,128,128]{2,1,0:T(8,128)} %bitcast.15, s32[1,10]{1,0:T(1,128)S(1)} %copy-done.4, s32[1,10]{1,0:T(1,128)S(1)} %copy-done.5, s32[3,1,10]{2,1,0:T(1,128)S(1)} %bitcast.17, ...), custom_call_target="tpu_custom_call" | custom-call | flops 1509949440 | bytes 819200 | tf_op jit(solution)/shard_map/pallas_call | solution.py:364
  68.5 0.0 copy-done
  68.5 0.0 copy-done.1
  68.5 0.8 %copy.16 = f32[1,10,128,128]{3,2,1,0:T(8,128)} copy(f32[1,10,128,128]{3,2,1,0:T(8,128)S(1)} %get-tuple-element.52) | data formatting | bytes 1310720
  69.4 0.8 %copy.17 = f32[1,10,128,128]{3,2,1,0:T(8,128)} copy(f32[1,10,128,128]{3,2,1,0:T(8,128)S(1)} %get-tuple-element.53) | data formatting | bytes 1310720
  (1 shorter events, 0.0 us)
Async XLA Ops:
  0.6 0.7 copy-start.5
  0.6 0.7 copy-start.2
  0.7 0.7 copy-start.3
  0.7 0.7 copy-start.4
  1.3 67.1 %copy-start = (f32[1,10,128,128]{3,2,1,0:T(8,128)S(1)}, f32[1,10,128,128]{3,2,1,0:T(8,128)}, u32[]{:S(2)}) copy-start(f32[1,10,128,128]{3,2,1,0:T(8,128)} %param.8) | copy-start | bytes 1966084
  1.3 67.2 %copy-start.1 = (f32[1,10,128,128]{3,2,1,0:T(8,128)S(1)}, f32[1,10,128,128]{3,2,1,0:T(8,128)}, u32[]{:S(2)}) copy-start(f32[1,10,128,128]{3,2,1,0:T(8,128)} %param.9) | copy-start | bytes 1966084

commit v3 on v2

--- a/solution.py
+++ b/solution.py
@@ -16,6 +16,9 @@
 OTHERS = 2
 WANT_MOST = SLOTS * OTHERS
 WANT_FEW = 8
+OFF_DIAG = 6
+TARGET = 32
+PLACES = 64
 
 
 def halves(x):
@@ -41,35 +44,25 @@
 
 
 def kernel(
-    cap,
-    d_ref, h_ref, rows_ref, cols_ref, left_ref, right_ref,
+    cap, dealt,
+    d_ref, h_ref, left_ref, right_ref,
     new_ref, ew_ref, over_ref,
-    pan_d, pan_q, own_h, deal_d, deal_h, deal_q, stage, got_d, got_h, got_q, mix_base, mix_dir, new_v, ew_v,
-    rows_s, cols_s, left_s, right_s, place_s, want_v, want_s, part, part_row, part_col,
+    pan_d, pan_q, own_d, own_h, own_q, pack, deal_d, deal_h, deal_q, stage, got_d, got_h, got_q, mix_base, mix_dir, new_v, ew_v,
+    mirror_stage, mirror_in, left_s, right_s, place_s, table_v, table_s, want_v, want_s, part, part_row, part_col,
     local_sem, near_send, near_recv, deal_send, deal_recv, got_send, got_recv,
-    want_send, want_recv, row_send, row_recv, col_send, col_recv,
+    want_send, want_recv, row_send, row_recv, col_send, col_recv, table_send, table_recv, mirror_send, mirror_recv,
 ):
     r, c = lax.axis_index("row"), lax.axis_index("col")
     up, down = lax.rem(c + 1, COLS), lax.rem(c + COLS - 1, COLS)
     first = r * SLOTS
     deal, got = (deal_d, deal_h, deal_q), (got_d, got_h, got_q)
-    own_d, own_q = pan_d.at[pl.ds(SLOTS, SLOTS)], pan_q.at[pl.ds(SLOTS, SLOTS)]
+    middle = pl.ds(SLOTS, SLOTS)
 
     def row_peer(step):
         return lax.rem(r + step, ROWS)
 
     def col_peer(step):
         return lax.rem(c + step, COLS)
-
-    barrier = pltpu.get_barrier_semaphore()
-
-    @pl.loop(1, ROWS)
-    def _(step):
-        pl.semaphore_signal(barrier, inc=1, device_id=(row_peer(step), c), device_id_type=MESH)
-
-    @pl.loop(1, COLS)
-    def _(step):
-        pl.semaphore_signal(barrier, inc=1, device_id=(r, col_peer(step)), device_id_type=MESH)
 
     loads = [
         pltpu.make_async_copy(src, dst, local_sem.at[k])
@@ -77,31 +70,55 @@
             (
                 (right_ref, right_s),
                 (d_ref, own_d),
+                (d_ref, pan_d.at[middle]),
                 (left_ref, left_s),
                 (h_ref, own_h),
-                (rows_ref, rows_s),
-                (cols_ref, cols_s),
             )
         )
     ]
     for load in loads:
         load.start()
+
+    barrier = pltpu.get_barrier_semaphore()
+
+    @pl.loop(1, ROWS)
+    def _(step):
+        pl.semaphore_signal(barrier, inc=1, device_id=(row_peer(step), c), device_id_type=MESH)
+
+    @pl.loop(1, COLS)
+    def _(step):
+        pl.semaphore_signal(barrier, inc=1, device_id=(r, col_peer(step)), device_id_type=MESH)
+
     loads[0].wait()
 
     lane = lax.broadcasted_iota(jnp.int32, (1, BS), 1)
-    wanted = jnp.zeros((1, BS), jnp.int32)
-    count = jnp.int32(0)
+    wanted = jnp.full((1, BS), PLACES, jnp.int32)
+    count, packed = jnp.int32(0), jnp.int32(0)
+    slots = [jnp.int32(p) for p in range(dealt)]
     for s in range(SLOTS):
         own = first + s
         one, two, three = (right_s[t, 0, s] for t in range(3))
+        lone = True
         for u, index in enumerate((jnp.where(one == own, two, one), jnp.where(three == own, two, three))):
             live = index >= 0
             near = index - first
             here = jnp.logical_and(near >= 0, near < SLOTS)
             away = jnp.logical_and(live, jnp.logical_not(here))
+            lone = jnp.logical_and(lone, jnp.logical_not(away))
             place_s[2 * s + u] = jnp.where(away, jnp.minimum(count, cap - 1), jnp.where(here, cap + near, 0))
-            wanted = jnp.where(lane == jnp.where(away, count, -1), index, wanted)
+            held = jnp.maximum(index, 0)
+            owner = lax.div(held, SLOTS)
+            address = owner * BS + PLACES + held - owner * SLOTS
+            wanted = jnp.where(lane == jnp.where(away, count, -1), address, wanted)
             count = count + away.astype(jnp.int32)
+        if dealt == SLOTS:
+            wanted = jnp.where(lane == PLACES + s, r * dealt + s, wanted)
+        else:
+            wanted = jnp.where(lane == PLACES + s, r * dealt + jnp.minimum(packed, dealt - 1), wanted)
+            here = jnp.where(lone, -1, packed)
+            for p in range(min(s + 1, dealt)):
+                slots[p] = jnp.where(here == p, s, slots[p])
+            packed = packed + jnp.logical_not(lone).astype(jnp.int32)
     want_v[r] = wanted
     over = jnp.where(count > cap, 1.0, 0.0)
 
@@ -118,10 +135,10 @@
             device_id=(peer, c), device_id_type=MESH,
         )
 
-    def deal_copy(k, own, src, dst, peer):
+    def deal_copy(k, src, dst, peer):
         return pltpu.make_async_remote_copy(
-            src_ref=own.at[:, pl.ds(pl.multiple_of(dst * CUT, CUT), CUT), :],
-            dst_ref=deal[k].at[pl.ds(src * SLOTS, SLOTS)],
+            src_ref=pack.at[k, :, pl.ds(pl.multiple_of(dst * CUT, CUT), CUT), :],
+            dst_ref=deal[k].at[pl.ds(src * dealt, dealt)],
             send_sem=deal_send.at[k, dst], recv_sem=deal_recv.at[k, src],
             device_id=(peer, c), device_id_type=MESH,
         )
@@ -146,25 +163,47 @@
         )
         return to_up, to_down
 
+    table_copies = [
+        pltpu.make_async_remote_copy(
+            src_ref=table_v.at[2], dst_ref=table_v.at[k], send_sem=table_send.at[k], recv_sem=table_recv.at[k],
+            device_id=(r, peer), device_id_type=MESH,
+        )
+        for k, peer in enumerate((up, down))
+    ]
+    mirror_copies = [
+        pltpu.make_async_remote_copy(
+            src_ref=mirror_stage.at[k], dst_ref=mirror_in.at[pl.ds(k * OFF_DIAG, OFF_DIAG)],
+            send_sem=mirror_send.at[k], recv_sem=mirror_recv.at[k],
+            device_id=(r, peer), device_id_type=MESH,
+        )
+        for k, peer in enumerate((up, down))
+    ]
+
     def deal_out(k, own):
+        for p in range(dealt):
+            pack[k, p] = own[slots[p]]
+
         @pl.loop(1, ROWS)
         def _(step):
             dst = row_peer(step)
-            deal_copy(k, own, r, dst, dst).start()
+            deal_copy(k, r, dst, dst).start()
 
         mine = pl.ds(pl.multiple_of(r * CUT, CUT), CUT)
+        for p in range(dealt):
+            deal[k][r * dealt + p] = pack[k, p, mine, :]
         for s in range(SLOTS):
-            deal[k][first + s] = own[s, mine, :]
             got[k][:, cap + s] = own[s].reshape(ROWS, CUT, BS)
 
-    def deal_in(k, own):
+    def deal_in(k):
         @pl.loop(1, ROWS)
         def _(step):
             src = row_peer(step)
-            deal_copy(k, own, src, r, src).wait_recv()
+            deal_copy(k, src, r, src).wait_recv()
 
     def pick(k, dst, q):
-        return deal[k][want_s[dst, 0, q]]
+        address = want_s[dst, 0, q]
+        row = lax.div(address, BS)
+        return deal[k][want_s[row, 0, address - row * BS]]
 
     def pass_on(k):
         @pl.loop(1, ROWS)
@@ -187,22 +226,61 @@
         places = (cap + s, place_s[2 * s], place_s[2 * s + 1])
         return right_operand([got[k][:, place].reshape(BS, BS) for place in places])
 
+    def by_term(s, values):
+        own = first + s
+        first_is, second_is, third_is = (right_s[t, 0, s] == own for t in range(3))
+        return (
+            jnp.where(first_is, values[0], jnp.where(second_is, values[1], values[2])),
+            jnp.where(first_is, values[1], values[0]),
+            jnp.where(third_is, values[1], values[2]),
+        )
+
+    def left_indices(s):
+        return by_term(s, [left_s[t, 0, s] for t in range(3)])
+
     def left_blocks(pan, s):
-        own = first + s
-        places = []
-        for t in range(3):
-            index = left_s[t, 0, s]
+        blocks = []
+        for index in left_indices(s):
             held = jnp.maximum(index, 0)
             owner = lax.div(held, SLOTS)
-            within = held - owner * SLOTS
             near = lax.rem(owner - c + 1 + COLS, COLS)
-            place = jnp.minimum(near * SLOTS + within, 3 * SLOTS)
-            places.append(jnp.where(index >= 0, place, 3 * SLOTS))
-        first_is, second_is, third_is = (right_s[t, 0, s] == own for t in range(3))
-        self_place = jnp.where(first_is, places[0], jnp.where(second_is, places[1], places[2]))
-        u0 = jnp.where(first_is, places[1], places[0])
-        u1 = jnp.where(third_is, places[1], places[2])
-        return left_operand([pan[self_place], pan[u0], pan[u1]])
+            place = jnp.minimum(near * SLOTS + held - owner * SLOTS, 3 * SLOTS)
+            blocks.append(pan[jnp.where(index >= 0, place, 3 * SLOTS)])
+        return left_operand(blocks)
+
+    def mirror_tables():
+        table = jnp.zeros((1, BS), jnp.int32)
+        to_up, to_down = table, table
+        ups, downs = jnp.int32(0), jnp.int32(0)
+        for s in range(SLOTS):
+            self_left, *others = left_indices(s)
+            diagonal = self_left == c * SLOTS + s
+            for u, index in enumerate(others):
+                e = 2 * s + u
+                side = lax.rem(lax.div(jnp.maximum(index, 0), SLOTS) - c + COLS, COLS)
+                live = jnp.logical_and(diagonal, index >= 0)
+                is_up = jnp.logical_and(live, side == 1)
+                is_down = jnp.logical_and(live, side == COLS - 1)
+                rank = jnp.minimum(jnp.where(is_up, ups, downs), OFF_DIAG - 1)
+                table = jnp.where(lane == e, rank, jnp.where(lane == TARGET + e, index, table))
+                to_up = jnp.where(lane == jnp.where(is_up, ups, -1), place_s[e], to_up)
+                to_down = jnp.where(lane == jnp.where(is_down, downs, -1), place_s[e], to_down)
+                ups, downs = ups + is_up.astype(jnp.int32), downs + is_down.astype(jnp.int32)
+        table_v[2] = table
+        table_v[3] = to_up
+        table_v[4] = to_down
+
+    def mirror(s):
+        self_left = left_indices(s)[0]
+        owner = lax.div(self_left, SLOTS)
+        e = 2 * (self_left - owner * SLOTS)
+        side = lax.rem(owner - c + COLS, COLS)
+        row = jnp.where(side == COLS - 1, 0, jnp.where(side == 1, 1, 2))
+        own = c * SLOTS + s
+        e = e + (table_s[row, 0, TARGET + e + 1] == own).astype(jnp.int32)
+        place = jnp.where(self_left == own, cap + s, place_s[e])
+        near = mirror_in[jnp.where(row == 2, 0, row * OFF_DIAG + table_s[row, 0, e])]
+        return jnp.where(row == 2, got_d[:, place].reshape(BS, BS), near)
 
     @pl.loop(1, ROWS)
     def _(step):
@@ -219,23 +297,33 @@
         src = row_peer(step)
         want_copy(src, r, src).wait_recv()
 
-    to_smem = pltpu.make_async_copy(want_v, want_s, local_sem.at[6])
+    to_smem = pltpu.make_async_copy(want_v, want_s, local_sem.at[5])
     to_smem.start()
     for load in loads[2:]:
         load.wait()
+    mirror_tables()
+    for copy in table_copies:
+        copy.start()
     to_smem.wait()
 
-    deal_in(0, own_d)
+    deal_in(0)
     pass_on(0)
     deal_out(1, own_h)
-    for copy in near_d:
+    for copy in (*table_copies, *near_d):
         copy.wait_recv()
+    tables_to_smem = pltpu.make_async_copy(table_v, table_s, local_sem.at[6])
+    tables_to_smem.start()
+    tables_to_smem.wait()
     get_in(0)
+    for k in range(2):
+        for q in range(OFF_DIAG):
+            mirror_stage[k, q] = got_d[:, table_s[3 + k, 0, q]].reshape(BS, BS)
+        mirror_copies[k].start()
 
     eye = lax.broadcasted_iota(jnp.int32, (BS, BS), 0) == lax.broadcasted_iota(jnp.int32, (BS, BS), 1)
 
     def trace_row(block, s):
-        on = (rows_s[0, s] == cols_s[0, s]).astype(jnp.float32)
+        on = (left_indices(s)[0] == c * SLOTS + s).astype(jnp.float32)
         return jnp.sum(jnp.where(eye, block, 0.0), axis=0, keepdims=True) * on
 
     part[...] = jnp.zeros_like(part)
@@ -244,30 +332,26 @@
     def _(s):
         square = product(left_blocks(pan_d, s), right_blocks(0, s))
         pan_q[SLOTS + s] = square
-        part[0:1, :] += trace_row(pan_d[SLOTS + s], s)
+        own_q[s] = square
+        part[0:1, :] += trace_row(own_d[s], s)
         part[1:2, :] += trace_row(square, s)
 
     near_q = near_copies(1, own_q, pan_q)
     deal_out(2, own_q)
     for copy in near_q:
         copy.start()
-    deal_in(1, own_h)
-    deal_in(2, own_q)
+    deal_in(1)
+    deal_in(2)
     pass_on(2)
-    pass_on(1)
-    for copy in near_q:
+    for copy in (*near_q, *mirror_copies):
         copy.wait_recv()
-    get_in(2)
 
     @pl.loop(0, SLOTS)
     def _(s):
-        square = pan_q[SLOTS + s]
-        both = product(left_blocks(pan_q, s), jnp.concatenate([right_blocks(0, s), right_blocks(2, s)], axis=1))
-        cube, fourth = both[:, :BS], both[:, BS:]
-        mix_base[s] = 4.0 * cube - 3.0 * fourth
-        mix_dir[s] = fourth - 2.0 * cube + square
+        cube = product(left_blocks(pan_q, s), right_blocks(0, s))
+        mix_dir[s] = cube
         part[2:3, :] += trace_row(cube, s)
-        part[3:4, :] += trace_row(fourth, s)
+        part[3:4, :] += jnp.sum(cube.T * mirror(s), axis=0, keepdims=True)
 
     part[4:5, :] = jnp.zeros((1, BS), jnp.float32) + over
 
@@ -289,6 +373,15 @@
         row_copy(r, dst, dst).start()
 
     part_row[r] = part[...]
+    pass_on(1)
+    get_in(2)
+
+    @pl.loop(0, SLOTS)
+    def _(s):
+        fourth = product(left_blocks(pan_q, s), right_blocks(2, s))
+        cube = mix_dir[s]
+        mix_base[s] = 4.0 * cube - 3.0 * fourth
+        mix_dir[s] = fourth - 2.0 * cube + own_q[s]
 
     @pl.loop(1, ROWS)
     def _(step):
@@ -331,7 +424,7 @@
     put_new = pltpu.make_async_copy(new_v, new_ref, local_sem.at[8])
     put_new.start()
 
-    for copy in (*near_d, *near_q):
+    for copy in (*near_d, *near_q, *table_copies, *mirror_copies):
         copy.wait_send()
 
     @pl.loop(1, ROWS)
@@ -339,8 +432,8 @@
         dst = row_peer(step)
         want_copy(r, dst, dst).wait_send()
         row_copy(r, dst, dst).wait_send()
-        for k, own in enumerate((own_d, own_h, own_q)):
-            deal_copy(k, own, r, dst, dst).wait_send()
+        for k in range(3):
+            deal_copy(k, r, dst, dst).wait_send()
             got_copy(k, r, dst, dst).wait_send()
 
     @pl.loop(1, COLS)
@@ -352,27 +445,30 @@
     put_new.wait()
 
 
-def step(cap, collective_id, *operands):
+def step(cap, dealt, collective_id, *operands):
     any_space = pl.BlockSpec(memory_space=pl.ANY)
     smem = pl.BlockSpec(memory_space=pltpu.SMEM)
     block = jax.ShapeDtypeStruct((SLOTS, BS, BS), jnp.float32)
     dma = pltpu.SemaphoreType.DMA
     panel = pltpu.VMEM((3 * SLOTS + 1, BS, BS), jnp.float32)
     own = pltpu.VMEM((SLOTS, BS, BS), jnp.float32)
-    dealt = pltpu.VMEM((ROWS * SLOTS, CUT, BS), jnp.float32)
+    slices = pltpu.VMEM((ROWS * dealt, CUT, BS), jnp.float32)
     fetched = pltpu.VMEM((ROWS, cap + SLOTS, CUT, BS), jnp.float32)
     return pl.pallas_call(
-        functools.partial(kernel, cap),
+        functools.partial(kernel, cap, dealt),
         out_shape=(block, block, jax.ShapeDtypeStruct((1, 1), jnp.float32)),
-        in_specs=[any_space] * 6,
+        in_specs=[any_space] * 4,
         out_specs=(any_space, any_space, smem),
         scratch_shapes=[
             panel,
             panel,
             own,
-            dealt,
-            dealt,
-            dealt,
+            own,
+            own,
+            pltpu.VMEM((3, dealt, BS, BS), jnp.float32),
+            slices,
+            slices,
+            slices,
             pltpu.VMEM((3, ROWS, cap, CUT, BS), jnp.float32),
             fetched,
             fetched,
@@ -381,11 +477,13 @@
             own,
             own,
             own,
-            pltpu.SMEM((1, SLOTS), jnp.int32),
-            pltpu.SMEM((1, SLOTS), jnp.int32),
+            pltpu.VMEM((2, OFF_DIAG, BS, BS), jnp.float32),
+            pltpu.VMEM((2 * OFF_DIAG, BS, BS), jnp.float32),
             pltpu.SMEM((3, 1, SLOTS), jnp.int32),
             pltpu.SMEM((3, 1, SLOTS), jnp.int32),
             pltpu.SMEM((WANT_MOST,), jnp.int32),
+            pltpu.VMEM((5, 1, BS), jnp.int32),
+            pltpu.SMEM((5, 1, BS), jnp.int32),
             pltpu.VMEM((ROWS, 1, BS), jnp.int32),
             pltpu.SMEM((ROWS, 1, BS), jnp.int32),
             pltpu.VMEM((8, BS), jnp.float32),
@@ -404,6 +502,10 @@
             dma((ROWS,)),
             dma((COLS,)),
             dma((COLS,)),
+            dma((2,)),
+            dma((2,)),
+            dma((2,)),
+            dma((2,)),
         ],
         compiler_params=pltpu.CompilerParams(
             collective_id=collective_id, has_side_effects=True, vmem_limit_bytes=60 * 1024 * 1024
@@ -415,13 +517,13 @@
 def shards(density, hamiltonian, block_rows, block_cols, left_index, right_index):
     terms_first = (2, 0, 1)
     operands = (
-        density[0], hamiltonian[0], block_rows, block_cols,
+        density[0], hamiltonian[0],
         jnp.transpose(left_index, terms_first), jnp.transpose(right_index, terms_first),
     )
-    new, ew, over = step(WANT_FEW, 0, *operands)
+    new, ew, over = step(WANT_FEW, min(WANT_FEW, SLOTS), 0, *operands)
     new, ew = lax.cond(
         over[0, 0] > 0.0,
-        lambda new, ew, *operands: tuple(step(WANT_MOST, 1, *operands)[:2]),
+        lambda new, ew, *operands: tuple(step(WANT_MOST, SLOTS, 1, *operands)[:2]),
         lambda new, ew, *operands: (new, ew),
         new, ew, *operands,
     )

time: 70.4 us -> 64.2 us (0.912)
  Pallas kernels: 66.5 us -> 60.3 us
    pallas_call x1, Pallas kernels: 66.5 us -> 60.3 us  [step(): pl.pallas_call(functools.partial(kernel, cap, dealt), out_shape=(block, b...]
    unnamed x14 -> x10, local copies, waits for them, and re-layouts: 2.36 us -> 2.36 us
where the time goes in v3:
time: 64.2 us; the launch traced here: 64.1 us
  Pallas kernels  60.3 us (94%)
  local copies, waits for them, and re-layouts  2.36 us (4%)
  between operations  1.36 us (2%)
    pallas_call x1, Pallas kernels, step(): pl.pallas_call(functools.partial(kernel, cap, dealt), out_shape=(block, b...  60.3 us
    unnamed x10, local copies, waits for them, and re-layouts  2.36 us

profile of v3, /device:TPU:1, one launch (start us, length us, event | category | flops | bytes accessed | tf_op | source)
XLA Modules:
  0.0 64.1 jit_solution(10184856398370322690)
XLA Ops:
  0.6 0.0 copy-start.2
  0.6 0.0 copy-start.3
  0.7 0.7 %copy-done.2 = s32[1,10,3]{1,0,2:T(1,128)S(1)} copy-done((s32[1,10,3]{1,0,2:T(1,128)S(1)}, s32[1,10,3]{1,0,2:T(1,128)}, u32[]{:S(2)}) %copy-start.2) | copy-done | bytes 144
  1.3 0.0 copy-done.3
  1.3 0.0 copy-start
  1.3 0.0 copy-start.1
  1.3 60.3 %shard_map.59 = (f32[10,128,128]{2,1,0:T(8,128)S(1)}, f32[10,128,128]{2,1,0:T(8,128)S(1)}, f32[1,1]{1,0:T(1,128)}) custom-call(f32[10,128,128]{2,1,0:T(8,128)} %bitcast.13, f32[10,128,128]{2,1,0:T(8,128)} %bitcast.15, s32[3,1,10]{2,1,0:T(1,128)S(1)} %bitcast.17, s32[3,1,10]{2,1,0:T(1,128)S(1)} %bitcast.19), custom_call_target="tpu_custom_call" | custom-call | flops 1509949440 | bytes 819200 | tf_op jit(solution)/shard_map/pallas_call | solution.py:457
  62.4 0.0 copy-done
  62.4 0.0 copy-done.1
  62.4 0.8 %copy.14 = f32[1,10,128,128]{3,2,1,0:T(8,128)} copy(f32[1,10,128,128]{3,2,1,0:T(8,128)S(1)} %get-tuple-element.46) | data formatting | bytes 1310720
  63.2 0.8 %copy.15 = f32[1,10,128,128]{3,2,1,0:T(8,128)} copy(f32[1,10,128,128]{3,2,1,0:T(8,128)S(1)} %get-tuple-element.47) | data formatting | bytes 1310720
  (1 shorter events, 0.0 us)
Async XLA Ops:
  0.6 0.7 %copy-start.2 = (s32[1,10,3]{1,0,2:T(1,128)S(1)}, s32[1,10,3]{1,0,2:T(1,128)}, u32[]{:S(2)}) copy-start(s32[1,10,3]{1,0,2:T(1,128)} %param.10) | copy-start | bytes 364
  0.6 0.7 %copy-start.3 = (s32[1,10,3]{1,0,2:T(1,128)S(1)}, s32[1,10,3]{1,0,2:T(1,128)}, u32[]{:S(2)}) copy-start(s32[1,10,3]{1,0,2:T(1,128)} %param.11) | copy-start | bytes 364
  1.3 61.0 %copy-start = (f32[1,10,128,128]{3,2,1,0:T(8,128)S(1)}, f32[1,10,128,128]{3,2,1,0:T(8,128)}, u32[]{:S(2)}) copy-start(f32[1,10,128,128]{3,2,1,0:T(8,128)} %param.8) | copy-start | bytes 1966084
  1.3 61.0 %copy-start.1 = (f32[1,10,128,128]{3,2,1,0:T(8,128)S(1)}, f32[1,10,128,128]{3,2,1,0:T(8,128)}, u32[]{:S(2)}) copy-start(f32[1,10,128,128]{3,2,1,0:T(8,128)} %param.9) | copy-start | bytes 1966084

commit v4 on v3

--- a/solution.py
+++ b/solution.py
@@ -18,6 +18,8 @@
 WANT_FEW = 8
 OFF_DIAG = 6
 TARGET = 32
+UNROLL = 10
+EARLY = 1
 PLACES = 64
 
 
@@ -44,12 +46,12 @@
 
 
 def kernel(
-    cap, dealt,
+    cap, dealt, quick,
     d_ref, h_ref, left_ref, right_ref,
     new_ref, ew_ref, over_ref,
-    pan_d, pan_q, own_d, own_h, own_q, pack, deal_d, deal_h, deal_q, stage, got_d, got_h, got_q, mix_base, mix_dir, new_v, ew_v,
+    pan_d, pan_q, own_d, own_h, own_q, pack, deal_d, deal_h, deal_q, stage, got_d, got_h, got_q, cube_v, turned_v, new_v, ew_v,
     mirror_stage, mirror_in, left_s, right_s, place_s, table_v, table_s, want_v, want_s, part, part_row, part_col,
-    local_sem, near_send, near_recv, deal_send, deal_recv, got_send, got_recv,
+    local_sem, put_sem, near_send, near_recv, deal_send, deal_recv, got_send, got_recv,
     want_send, want_recv, row_send, row_recv, col_send, col_recv, table_send, table_recv, mirror_send, mirror_recv,
 ):
     r, c = lax.axis_index("row"), lax.axis_index("col")
@@ -120,7 +122,6 @@
                 slots[p] = jnp.where(here == p, s, slots[p])
             packed = packed + jnp.logical_not(lone).astype(jnp.int32)
     want_v[r] = wanted
-    over = jnp.where(count > cap, 1.0, 0.0)
 
     zero_block = jnp.zeros((BS, BS), jnp.float32)
     pan_d[3 * SLOTS] = zero_block
@@ -205,16 +206,17 @@
         row = lax.div(address, BS)
         return deal[k][want_s[row, 0, address - row * BS]]
 
-    def pass_on(k):
-        @pl.loop(1, ROWS)
+    def pass_on(k, low, high):
+        @pl.loop(low, high)
         def _(step):
             dst = row_peer(step)
             for q in range(cap):
                 stage[k, dst, q] = pick(k, dst, q)
             got_copy(k, r, dst, dst).start()
 
-        for q in range(cap):
-            got[k][r, q] = pick(k, r, q)
+        if high == ROWS:
+            for q in range(cap):
+                got[k][r, q] = pick(k, r, q)
 
     def get_in(k):
         @pl.loop(1, ROWS)
@@ -238,23 +240,26 @@
     def left_indices(s):
         return by_term(s, [left_s[t, 0, s] for t in range(3)])
 
+    def panel_block(pan, index):
+        held = jnp.maximum(index, 0)
+        owner = lax.div(held, SLOTS)
+        near = lax.rem(owner - c + 1 + COLS, COLS)
+        place = jnp.minimum(near * SLOTS + held - owner * SLOTS, 3 * SLOTS)
+        return pan[jnp.where(index >= 0, place, 3 * SLOTS)]
+
     def left_blocks(pan, s):
-        blocks = []
-        for index in left_indices(s):
-            held = jnp.maximum(index, 0)
-            owner = lax.div(held, SLOTS)
-            near = lax.rem(owner - c + 1 + COLS, COLS)
-            place = jnp.minimum(near * SLOTS + held - owner * SLOTS, 3 * SLOTS)
-            blocks.append(pan[jnp.where(index >= 0, place, 3 * SLOTS)])
-        return left_operand(blocks)
+        return left_operand([panel_block(pan, index) for index in left_indices(s)])
 
     def mirror_tables():
+        threes = jnp.int32(0)
         table = jnp.zeros((1, BS), jnp.int32)
         to_up, to_down = table, table
         ups, downs = jnp.int32(0), jnp.int32(0)
         for s in range(SLOTS):
             self_left, *others = left_indices(s)
             diagonal = self_left == c * SLOTS + s
+            three = jnp.logical_and(jnp.logical_not(diagonal), others[1] >= 0)
+            threes = threes + three.astype(jnp.int32)
             for u, index in enumerate(others):
                 e = 2 * s + u
                 side = lax.rem(lax.div(jnp.maximum(index, 0), SLOTS) - c + COLS, COLS)
@@ -269,6 +274,7 @@
         table_v[2] = table
         table_v[3] = to_up
         table_v[4] = to_down
+        return threes
 
     def mirror(s):
         self_left = left_indices(s)[0]
@@ -301,13 +307,14 @@
     to_smem.start()
     for load in loads[2:]:
         load.wait()
-    mirror_tables()
+    threes = mirror_tables()
+    over = jnp.where(jnp.logical_or(count > cap, threes > 0), 1.0, 0.0)
     for copy in table_copies:
         copy.start()
     to_smem.wait()
 
     deal_in(0)
-    pass_on(0)
+    pass_on(0, 1, ROWS)
     deal_out(1, own_h)
     for copy in (*table_copies, *near_d):
         copy.wait_recv()
@@ -328,7 +335,7 @@
 
     part[...] = jnp.zeros_like(part)
 
-    @pl.loop(0, SLOTS)
+    @pl.loop(0, SLOTS, unroll=UNROLL)
     def _(s):
         square = product(left_blocks(pan_d, s), right_blocks(0, s))
         pan_q[SLOTS + s] = square
@@ -336,93 +343,139 @@
         part[0:1, :] += trace_row(own_d[s], s)
         part[1:2, :] += trace_row(square, s)
 
+    def row_copy(src, dst, peer):
+        return pltpu.make_async_remote_copy(
+            src_ref=part, dst_ref=part_row.at[src], send_sem=row_send.at[dst], recv_sem=row_recv.at[src],
+            device_id=(peer, c), device_id_type=MESH,
+        )
+
+    def col_copy(src, dst, peer):
+        return pltpu.make_async_remote_copy(
+            src_ref=part_col.at[src], dst_ref=part_col.at[src], send_sem=col_send.at[dst], recv_sem=col_recv.at[src],
+            device_id=(r, peer), device_id_type=MESH,
+        )
+
+    def sum_rows_start():
+        part[4:5, :] = jnp.zeros((1, BS), jnp.float32) + over
+
+        @pl.loop(1, ROWS)
+        def _(step):
+            dst = row_peer(step)
+            row_copy(r, dst, dst).start()
+
+        part_row[r] = part[...]
+
+    def sum_cols_start():
+        @pl.loop(1, ROWS)
+        def _(step):
+            src = row_peer(step)
+            row_copy(src, r, src).wait_recv()
+
+        part_col[c] = jnp.sum(part_row[...], axis=0)
+
+        @pl.loop(1, COLS)
+        def _(step):
+            dst = col_peer(step)
+            col_copy(c, dst, dst).start()
+
+    def trace_factors():
+        @pl.loop(0, SLOTS, unroll=UNROLL)
+        def _(s):
+            square = own_q[s]
+            turned = square.T
+            self_left = left_indices(s)[0]
+            corner = got_d[:, place_s[2 * s]].reshape(BS, BS)
+            left = left_operand([square, panel_block(pan_d, self_left)])
+            factor = product(left, right_operand([corner, square]))
+            on = self_left == c * SLOTS + s
+            turned_v[0, s] = turned
+            turned_v[1, s] = jnp.where(on, 0.0, factor.T)
+            part[3:4, :] += jnp.sum(jnp.where(on, turned * square, 0.0), axis=0, keepdims=True)
+
+    def traces_without_triangles():
+        @pl.loop(0, SLOTS, unroll=UNROLL)
+        def _(s):
+            back = mirror(s)
+            part[2:3, :] += jnp.sum(turned_v[0, s] * back, axis=0, keepdims=True)
+            part[3:4, :] += jnp.sum(turned_v[1, s] * back, axis=0, keepdims=True)
+
+    def find_gamma():
+        @pl.loop(1, COLS)
+        def _(step):
+            src = col_peer(step)
+            col_copy(src, c, src).wait_recv()
+
+        sums = jnp.sum(part_col[...], axis=0)
+        over_ref[0, 0] = jnp.sum(sums[4:5, :])
+        traces = jnp.sum(sums, axis=1, keepdims=True)
+        one, two, three, four = (traces[k : k + 1, :] for k in range(4))
+        trace_f = 4.0 * three - 3.0 * four
+        trace_g = four - 2.0 * three + two
+        return jnp.clip((one - trace_f) / jnp.maximum(jnp.abs(trace_g), 1.0), 0.0, 6.0)
+
+    def put(k, src, dst, s):
+        return pltpu.make_async_copy(src.at[s], dst.at[s], put_sem.at[k, s])
+
+    def make_cube():
+        @pl.loop(0, SLOTS, unroll=UNROLL)
+        def _(s):
+            cube = product(left_blocks(pan_q, s), right_blocks(0, s))
+            cube_v[s] = cube
+            if not quick:
+                part[2:3, :] += trace_row(cube, s)
+                part[3:4, :] += jnp.sum(cube.T * mirror(s), axis=0, keepdims=True)
+
+    def make_new(gamma):
+        @pl.loop(0, SLOTS, unroll=UNROLL)
+        def _(s):
+            fourth = product(left_blocks(pan_q, s), right_blocks(2, s))
+            cube = cube_v[s]
+            new_v[s] = 4.0 * cube - 3.0 * fourth + gamma * (fourth - 2.0 * cube + own_q[s])
+            put(0, new_v, new_ref, s).start()
+
+    def make_energy():
+        @pl.loop(0, SLOTS, unroll=UNROLL)
+        def _(s):
+            ew_v[s] = product(left_blocks(pan_q, s), right_blocks(1, s))
+            put(1, ew_v, ew_ref, s).start()
+
     near_q = near_copies(1, own_q, pan_q)
     deal_out(2, own_q)
     for copy in near_q:
         copy.start()
+    if quick:
+        trace_factors()
+        for copy in mirror_copies:
+            copy.wait_recv()
+        traces_without_triangles()
+        sum_rows_start()
     deal_in(1)
+    pass_on(1, 1, EARLY)
     deal_in(2)
-    pass_on(2)
-    for copy in (*near_q, *mirror_copies):
+    pass_on(2, 1, ROWS)
+    pass_on(1, EARLY, ROWS)
+    if quick:
+        sum_cols_start()
+    else:
+        for copy in mirror_copies:
+            copy.wait_recv()
+    for copy in near_q:
         copy.wait_recv()
-
-    @pl.loop(0, SLOTS)
-    def _(s):
-        cube = product(left_blocks(pan_q, s), right_blocks(0, s))
-        mix_dir[s] = cube
-        part[2:3, :] += trace_row(cube, s)
-        part[3:4, :] += jnp.sum(cube.T * mirror(s), axis=0, keepdims=True)
-
-    part[4:5, :] = jnp.zeros((1, BS), jnp.float32) + over
-
-    def row_copy(src, dst, peer):
-        return pltpu.make_async_remote_copy(
-            src_ref=part, dst_ref=part_row.at[src], send_sem=row_send.at[dst], recv_sem=row_recv.at[src],
-            device_id=(peer, c), device_id_type=MESH,
-        )
-
-    def col_copy(src, dst, peer):
-        return pltpu.make_async_remote_copy(
-            src_ref=part_col.at[src], dst_ref=part_col.at[src], send_sem=col_send.at[dst], recv_sem=col_recv.at[src],
-            device_id=(r, peer), device_id_type=MESH,
-        )
-
-    @pl.loop(1, ROWS)
-    def _(step):
-        dst = row_peer(step)
-        row_copy(r, dst, dst).start()
-
-    part_row[r] = part[...]
-    pass_on(1)
-    get_in(2)
-
-    @pl.loop(0, SLOTS)
-    def _(s):
-        fourth = product(left_blocks(pan_q, s), right_blocks(2, s))
-        cube = mix_dir[s]
-        mix_base[s] = 4.0 * cube - 3.0 * fourth
-        mix_dir[s] = fourth - 2.0 * cube + own_q[s]
-
-    @pl.loop(1, ROWS)
-    def _(step):
-        src = row_peer(step)
-        row_copy(src, r, src).wait_recv()
-
-    part_col[c] = jnp.sum(part_row[...], axis=0)
-
-    @pl.loop(1, COLS)
-    def _(step):
-        dst = col_peer(step)
-        col_copy(c, dst, dst).start()
-
-    get_in(1)
-
-    @pl.loop(0, SLOTS)
-    def _(s):
-        ew_v[s] = product(left_blocks(pan_q, s), right_blocks(1, s))
-
-    put_ew = pltpu.make_async_copy(ew_v, ew_ref, local_sem.at[7])
-    put_ew.start()
-
-    @pl.loop(1, COLS)
-    def _(step):
-        src = col_peer(step)
-        col_copy(src, c, src).wait_recv()
-
-    sums = jnp.sum(part_col[...], axis=0)
-    over_ref[0, 0] = jnp.sum(sums[4:5, :])
-    traces = jnp.sum(sums, axis=1, keepdims=True)
-    one, two, three, four = (traces[k : k + 1, :] for k in range(4))
-    trace_f = 4.0 * three - 3.0 * four
-    trace_g = four - 2.0 * three + two
-    gamma = jnp.clip((one - trace_f) / jnp.maximum(jnp.abs(trace_g), 1.0), 0.0, 6.0)
-
-    @pl.loop(0, SLOTS)
-    def _(s):
-        new_v[s] = mix_base[s] + gamma * mix_dir[s]
-
-    put_new = pltpu.make_async_copy(new_v, new_ref, local_sem.at[8])
-    put_new.start()
+    make_cube()
+    if not quick:
+        sum_rows_start()
+        sum_cols_start()
+    gamma = find_gamma()
+    if EARLY == ROWS:
+        get_in(1)
+        make_energy()
+        get_in(2)
+        make_new(gamma)
+    else:
+        get_in(2)
+        make_new(gamma)
+        get_in(1)
+        make_energy()
 
     for copy in (*near_d, *near_q, *table_copies, *mirror_copies):
         copy.wait_send()
@@ -441,11 +494,13 @@
         dst = col_peer(step)
         col_copy(c, dst, dst).wait_send()
 
-    put_ew.wait()
-    put_new.wait()
-
-
-def step(cap, dealt, collective_id, *operands):
+    @pl.loop(0, SLOTS)
+    def _(s):
+        put(0, new_v, new_ref, s).wait()
+        put(1, ew_v, ew_ref, s).wait()
+
+
+def step(cap, dealt, quick, collective_id, *operands):
     any_space = pl.BlockSpec(memory_space=pl.ANY)
     smem = pl.BlockSpec(memory_space=pltpu.SMEM)
     block = jax.ShapeDtypeStruct((SLOTS, BS, BS), jnp.float32)
@@ -455,7 +510,7 @@
     slices = pltpu.VMEM((ROWS * dealt, CUT, BS), jnp.float32)
     fetched = pltpu.VMEM((ROWS, cap + SLOTS, CUT, BS), jnp.float32)
     return pl.pallas_call(
-        functools.partial(kernel, cap, dealt),
+        functools.partial(kernel, cap, dealt, quick),
         out_shape=(block, block, jax.ShapeDtypeStruct((1, 1), jnp.float32)),
         in_specs=[any_space] * 4,
         out_specs=(any_space, any_space, smem),
@@ -474,7 +529,7 @@
             fetched,
             fetched,
             own,
-            own,
+            pltpu.VMEM((2, SLOTS, BS, BS), jnp.float32),
             own,
             own,
             pltpu.VMEM((2, OFF_DIAG, BS, BS), jnp.float32),
@@ -490,6 +545,7 @@
             pltpu.VMEM((ROWS, 8, BS), jnp.float32),
             pltpu.VMEM((COLS, 8, BS), jnp.float32),
             dma((9,)),
+            dma((2, SLOTS)),
             dma((2, 2)),
             dma((2, 2)),
             dma((3, ROWS)),
@@ -520,10 +576,10 @@
         density[0], hamiltonian[0],
         jnp.transpose(left_index, terms_first), jnp.transpose(right_index, terms_first),
     )
-    new, ew, over = step(WANT_FEW, min(WANT_FEW, SLOTS), 0, *operands)
+    new, ew, over = step(WANT_FEW, min(WANT_FEW, SLOTS), True, 0, *operands)
     new, ew = lax.cond(
         over[0, 0] > 0.0,
-        lambda new, ew, *operands: tuple(step(WANT_MOST, SLOTS, 1, *operands)[:2]),
+        lambda new, ew, *operands: tuple(step(WANT_MOST, SLOTS, False, 1, *operands)[:2]),
         lambda new, ew, *operands: (new, ew),
         new, ew, *operands,
     )

time: 64.2 us -> 60.7 us (0.945)
  Pallas kernels: 60.3 us -> 56.6 us
    pallas_call x1, Pallas kernels: 60.3 us -> 56.6 us  [step(): pl.pallas_call(functools.partial(kernel, cap, dealt, quick), out_shape=(b...]
where the time goes in v4:
time: 60.7 us; the launch traced here: 60.6 us
  Pallas kernels  56.6 us (93%)
  local copies, waits for them, and re-layouts  2.36 us (4%)
  between operations  1.36 us (2%)
    pallas_call x1, Pallas kernels, step(): pl.pallas_call(functools.partial(kernel, cap, dealt, quick), out_shape=(b...  56.6 us
    unnamed x10, local copies, waits for them, and re-layouts  2.36 us

profile of v4, /device:TPU:1, one launch (start us, length us, event | category | flops | bytes accessed | tf_op | source)
XLA Modules:
  0.0 60.6 jit_solution(3455030894539472419)
XLA Ops:
  0.6 0.0 copy-start.2
  0.6 0.0 copy-start.3
  0.7 0.7 %copy-done.2 = s32[1,10,3]{1,0,2:T(1,128)S(1)} copy-done((s32[1,10,3]{1,0,2:T(1,128)S(1)}, s32[1,10,3]{1,0,2:T(1,128)}, u32[]{:S(2)}) %copy-start.2) | copy-done | bytes 144
  1.3 0.0 copy-done.3
  1.3 0.0 copy-start
  1.3 0.0 copy-start.1
  1.3 56.6 %shard_map.59 = (f32[10,128,128]{2,1,0:T(8,128)S(1)}, f32[10,128,128]{2,1,0:T(8,128)S(1)}, f32[1,1]{1,0:T(1,128)}) custom-call(f32[10,128,128]{2,1,0:T(8,128)} %bitcast.13, f32[10,128,128]{2,1,0:T(8,128)} %bitcast.15, s32[3,1,10]{2,1,0:T(1,128)S(1)} %bitcast.17, s32[3,1,10]{2,1,0:T(1,128)S(1)} %bitcast.19), custom_call_target="tpu_custom_call" | custom-call | flops 1509949440 | bytes 819200 | tf_op jit(solution)/shard_map/pallas_call | solution.py:512
  58.7 0.0 copy-done
  58.7 0.0 copy-done.1
  58.7 0.2 conditional.1
  58.9 0.8 %copy.14 = f32[1,10,128,128]{3,2,1,0:T(8,128)} copy(f32[1,10,128,128]{3,2,1,0:T(8,128)S(1)} %get-tuple-element.46) | data formatting | bytes 1310720
  59.7 0.8 %copy.15 = f32[1,10,128,128]{3,2,1,0:T(8,128)} copy(f32[1,10,128,128]{3,2,1,0:T(8,128)S(1)} %get-tuple-element.47) | data formatting | bytes 1310720
Async XLA Ops:
  0.6 0.7 %copy-start.2 = (s32[1,10,3]{1,0,2:T(1,128)S(1)}, s32[1,10,3]{1,0,2:T(1,128)}, u32[]{:S(2)}) copy-start(s32[1,10,3]{1,0,2:T(1,128)} %param.10) | copy-start | bytes 364
  0.6 0.7 %copy-start.3 = (s32[1,10,3]{1,0,2:T(1,128)S(1)}, s32[1,10,3]{1,0,2:T(1,128)}, u32[]{:S(2)}) copy-start(s32[1,10,3]{1,0,2:T(1,128)} %param.11) | copy-start | bytes 364
  1.3 57.3 %copy-start = (f32[1,10,128,128]{3,2,1,0:T(8,128)S(1)}, f32[1,10,128,128]{3,2,1,0:T(8,128)}, u32[]{:S(2)}) copy-start(f32[1,10,128,128]{3,2,1,0:T(8,128)} %param.8) | copy-start | bytes 1966084
  1.3 57.3 %copy-start.1 = (f32[1,10,128,128]{3,2,1,0:T(8,128)S(1)}, f32[1,10,128,128]{3,2,1,0:T(8,128)}, u32[]{:S(2)}) copy-start(f32[1,10,128,128]{3,2,1,0:T(8,128)} %param.9) | copy-start | bytes 1966084

commit v5 on v4

--- a/solution.py
+++ b/solution.py
@@ -19,7 +19,7 @@
 OFF_DIAG = 6
 TARGET = 32
 UNROLL = 10
-EARLY = 1
+EARLY = ROWS
 PLACES = 64
 
 
@@ -49,9 +49,9 @@
     cap, dealt, quick,
     d_ref, h_ref, left_ref, right_ref,
     new_ref, ew_ref, over_ref,
-    pan_d, pan_q, own_d, own_h, own_q, pack, deal_d, deal_h, deal_q, stage, got_d, got_h, got_q, cube_v, turned_v, new_v, ew_v,
+    pan_d, pan_q, own_d, own_h, own_q, pack, deal_d, deal_h, deal_q, stage, got_d, got_h, got_q, cube_v, turned_v,
     mirror_stage, mirror_in, left_s, right_s, place_s, table_v, table_s, want_v, want_s, part, part_row, part_col,
-    local_sem, put_sem, near_send, near_recv, deal_send, deal_recv, got_send, got_recv,
+    local_sem, near_send, near_recv, deal_send, deal_recv, got_send, got_recv,
     want_send, want_recv, row_send, row_recv, col_send, col_recv, table_send, table_recv, mirror_send, mirror_recv,
 ):
     r, c = lax.axis_index("row"), lax.axis_index("col")
@@ -413,9 +413,6 @@
         trace_g = four - 2.0 * three + two
         return jnp.clip((one - trace_f) / jnp.maximum(jnp.abs(trace_g), 1.0), 0.0, 6.0)
 
-    def put(k, src, dst, s):
-        return pltpu.make_async_copy(src.at[s], dst.at[s], put_sem.at[k, s])
-
     def make_cube():
         @pl.loop(0, SLOTS, unroll=UNROLL)
         def _(s):
@@ -430,14 +427,12 @@
         def _(s):
             fourth = product(left_blocks(pan_q, s), right_blocks(2, s))
             cube = cube_v[s]
-            new_v[s] = 4.0 * cube - 3.0 * fourth + gamma * (fourth - 2.0 * cube + own_q[s])
-            put(0, new_v, new_ref, s).start()
+            new_ref[s] = 4.0 * cube - 3.0 * fourth + gamma * (fourth - 2.0 * cube + own_q[s])
 
     def make_energy():
         @pl.loop(0, SLOTS, unroll=UNROLL)
         def _(s):
-            ew_v[s] = product(left_blocks(pan_q, s), right_blocks(1, s))
-            put(1, ew_v, ew_ref, s).start()
+            ew_ref[s] = product(left_blocks(pan_q, s), right_blocks(1, s))
 
     near_q = near_copies(1, own_q, pan_q)
     deal_out(2, own_q)
@@ -494,15 +489,11 @@
         dst = col_peer(step)
         col_copy(c, dst, dst).wait_send()
 
-    @pl.loop(0, SLOTS)
-    def _(s):
-        put(0, new_v, new_ref, s).wait()
-        put(1, ew_v, ew_ref, s).wait()
-
 
 def step(cap, dealt, quick, collective_id, *operands):
     any_space = pl.BlockSpec(memory_space=pl.ANY)
     smem = pl.BlockSpec(memory_space=pltpu.SMEM)
+    vmem = pl.BlockSpec(memory_space=pltpu.VMEM)
     block = jax.ShapeDtypeStruct((SLOTS, BS, BS), jnp.float32)
     dma = pltpu.SemaphoreType.DMA
     panel = pltpu.VMEM((3 * SLOTS + 1, BS, BS), jnp.float32)
@@ -513,7 +504,7 @@
         functools.partial(kernel, cap, dealt, quick),
         out_shape=(block, block, jax.ShapeDtypeStruct((1, 1), jnp.float32)),
         in_specs=[any_space] * 4,
-        out_specs=(any_space, any_space, smem),
+        out_specs=(vmem, vmem, smem),
         scratch_shapes=[
             panel,
             panel,
@@ -530,8 +521,6 @@
             fetched,
             own,
             pltpu.VMEM((2, SLOTS, BS, BS), jnp.float32),
-            own,
-            own,
             pltpu.VMEM((2, OFF_DIAG, BS, BS), jnp.float32),
             pltpu.VMEM((2 * OFF_DIAG, BS, BS), jnp.float32),
             pltpu.SMEM((3, 1, SLOTS), jnp.int32),
@@ -545,7 +534,6 @@
             pltpu.VMEM((ROWS, 8, BS), jnp.float32),
             pltpu.VMEM((COLS, 8, BS), jnp.float32),
             dma((9,)),
-            dma((2, SLOTS)),
             dma((2, 2)),
             dma((2, 2)),
             dma((3, ROWS)),
@@ -570,6 +558,27 @@
     )(*operands)
 
 
+def write_kernel(new_in, ew_in, new_ref, ew_ref, sem):
+    pairs = ((new_in, new_ref), (ew_in, ew_ref))
+    copies = [pltpu.make_async_copy(src, dst, sem.at[k]) for k, (src, dst) in enumerate(pairs)]
+    for copy in copies:
+        copy.start()
+    for copy in copies:
+        copy.wait()
+
+
+def write_out(new, ew):
+    any_space = pl.BlockSpec(memory_space=pl.ANY)
+    block = jax.ShapeDtypeStruct((SLOTS, BS, BS), jnp.float32)
+    return pl.pallas_call(
+        write_kernel,
+        out_shape=(block, block),
+        in_specs=[any_space, any_space],
+        out_specs=(any_space, any_space),
+        scratch_shapes=[pltpu.SemaphoreType.DMA((2,))],
+    )(new, ew)
+
+
 def shards(density, hamiltonian, block_rows, block_cols, left_index, right_index):
     terms_first = (2, 0, 1)
     operands = (
@@ -583,6 +592,7 @@
         lambda new, ew, *operands: (new, ew),
         new, ew, *operands,
     )
+    new, ew = write_out(new, ew)
     return new[None], ew[None]
 
 

time: 60.7 us -> 55.9 us (0.921)
  Pallas kernels: 56.6 us -> 53.4 us
  local copies, waits for them, and re-layouts: 2.36 us -> 0.69 us
    pallas_call x1, Pallas kernels: 56.6 us -> 52.3 us  [step(): pl.pallas_call(functools.partial(kernel, cap, dealt, quick), out_shape=(b...]
    unnamed x10 -> x8, local copies, waits for them, and re-layouts: 2.36 us -> 0.69 us
    pallas_call x0 -> x1, Pallas kernels: none -> 1.07 us  [write_out(): pl.pallas_call(write_kernel, out_shape=(block, block), in_specs=[any_spac...]
where the time goes in v5:
time: 55.9 us; the launch traced here: 55.7 us
  Pallas kernels  53.4 us (96%)
  between operations  1.47 us (3%)
  local copies, waits for them, and re-layouts  0.69 us (1%)
    pallas_call x1, Pallas kernels, step(): pl.pallas_call(functools.partial(kernel, cap, dealt, quick), out_shape=(b...  52.3 us

profile of v5, /device:TPU:1, one launch (start us, length us, event | category | flops | bytes accessed | tf_op | source)
XLA Modules:
  0.0 55.7 jit_solution(17447697400821990245)
XLA Ops:
  0.6 0.0 copy-start.2
  0.6 0.0 copy-start.3
  0.7 0.7 %copy-done.2 = s32[1,10,3]{1,0,2:T(1,128)S(1)} copy-done((s32[1,10,3]{1,0,2:T(1,128)S(1)}, s32[1,10,3]{1,0,2:T(1,128)}, u32[]{:S(2)}) %copy-start.2) | copy-done | bytes 144
  1.3 0.0 copy-done.3
  1.3 0.0 copy-start
  1.3 0.0 copy-start.1
  1.3 52.3 %shard_map.59 = (f32[10,128,128]{2,1,0:T(8,128)S(1)}, f32[10,128,128]{2,1,0:T(8,128)S(1)}, f32[1,1]{1,0:T(1,128)}) custom-call(f32[10,128,128]{2,1,0:T(8,128)} %bitcast.7, f32[10,128,128]{2,1,0:T(8,128)} %bitcast.9, s32[3,1,10]{2,1,0:T(1,128)S(1)} %bitcast.13, s32[3,1,10]{2,1,0:T(1,128)S(1)} %bitcast.15), custom_call_target="tpu_custom_call" | custom-call | flops 1509949440 | bytes 819200 | tf_op jit(solution)/shard_map/pallas_call | solution.py:503
  54.3 0.0 copy-done
  54.3 0.0 copy-done.1
  54.3 0.2 conditional.1
  54.5 1.1 %shard_map.60 = (f32[10,128,128]{2,1,0:T(8,128)}, f32[10,128,128]{2,1,0:T(8,128)}) custom-call(f32[10,128,128]{2,1,0:T(8,128)S(1)} %get-tuple-element.30.new_in, f32[10,128,128]{2,1,0:T(8,128)S(1)} %get-tuple-element.31.ew_in), custom_call_target="tpu_custom_call" | custom-call | tf_op jit(solution)/shard_map/pallas_call | solution.py:573
Async XLA Ops:
  0.6 0.7 %copy-start.2 = (s32[1,10,3]{1,0,2:T(1,128)S(1)}, s32[1,10,3]{1,0,2:T(1,128)}, u32[]{:S(2)}) copy-start(s32[1,10,3]{1,0,2:T(1,128)} %param.10) | copy-start | bytes 364
  0.6 0.7 %copy-start.3 = (s32[1,10,3]{1,0,2:T(1,128)S(1)}, s32[1,10,3]{1,0,2:T(1,128)}, u32[]{:S(2)}) copy-start(s32[1,10,3]{1,0,2:T(1,128)} %param.11) | copy-start | bytes 364
  1.3 53.0 %copy-start = (f32[1,10,128,128]{3,2,1,0:T(8,128)S(1)}, f32[1,10,128,128]{3,2,1,0:T(8,128)}, u32[]{:S(2)}) copy-start(f32[1,10,128,128]{3,2,1,0:T(8,128)} %param.8) | copy-start | bytes 1966084
  1.3 53.0 %copy-start.1 = (f32[1,10,128,128]{3,2,1,0:T(8,128)S(1)}, f32[1,10,128,128]{3,2,1,0:T(8,128)}, u32[]{:S(2)}) copy-start(f32[1,10,128,128]{3,2,1,0:T(8,128)} %param.9) | copy-start | bytes 1966084

commit v6 on v5

--- a/solution.py
+++ b/solution.py
@@ -130,9 +130,30 @@
 
     pl.semaphore_wait(barrier, ROWS + COLS - 2)
 
+    def all_of(ref, count, send_sem, recv_sem):
+        some = ref.at[pl.ds(0, count)]
+        return pltpu.make_async_remote_copy(
+            src_ref=some, dst_ref=some, send_sem=send_sem, recv_sem=recv_sem, device_id=(r, up), device_id_type=MESH
+        )
+
+    def all_wants():
+        return all_of(want_v, ROWS - 1, want_send, want_recv)
+
+    def all_dealt(k):
+        return all_of(deal[k], (ROWS - 1) * dealt, deal_send.at[k], deal_recv.at[k])
+
+    def all_got(k):
+        return all_of(stage.at[k], ROWS - 1, got_send.at[k], got_recv.at[k])
+
+    def all_rows():
+        return all_of(part_row, ROWS - 1, row_send, row_recv)
+
+    def all_cols():
+        return all_of(part_col, COLS - 1, col_send, col_recv)
+
     def want_copy(src, dst, peer):
         return pltpu.make_async_remote_copy(
-            src_ref=want_v.at[src], dst_ref=want_v.at[src], send_sem=want_send.at[dst], recv_sem=want_recv.at[src],
+            src_ref=want_v.at[src], dst_ref=want_v.at[src], send_sem=want_send, recv_sem=want_recv,
             device_id=(peer, c), device_id_type=MESH,
         )
 
@@ -140,14 +161,14 @@
         return pltpu.make_async_remote_copy(
             src_ref=pack.at[k, :, pl.ds(pl.multiple_of(dst * CUT, CUT), CUT), :],
             dst_ref=deal[k].at[pl.ds(src * dealt, dealt)],
-            send_sem=deal_send.at[k, dst], recv_sem=deal_recv.at[k, src],
+            send_sem=deal_send.at[k], recv_sem=deal_recv.at[k],
             device_id=(peer, c), device_id_type=MESH,
         )
 
     def got_copy(k, src, dst, peer):
         return pltpu.make_async_remote_copy(
             src_ref=stage.at[k, dst], dst_ref=got[k].at[src, pl.ds(0, cap)],
-            send_sem=got_send.at[k, dst], recv_sem=got_recv.at[k, src],
+            send_sem=got_send.at[k], recv_sem=got_recv.at[k],
             device_id=(peer, c), device_id_type=MESH,
         )
 
@@ -196,10 +217,7 @@
             got[k][:, cap + s] = own[s].reshape(ROWS, CUT, BS)
 
     def deal_in(k):
-        @pl.loop(1, ROWS)
-        def _(step):
-            src = row_peer(step)
-            deal_copy(k, src, r, src).wait_recv()
+        all_dealt(k).wait_recv()
 
     def pick(k, dst, q):
         address = want_s[dst, 0, q]
@@ -219,10 +237,7 @@
                 got[k][r, q] = pick(k, r, q)
 
     def get_in(k):
-        @pl.loop(1, ROWS)
-        def _(step):
-            src = row_peer(step)
-            got_copy(k, src, r, src).wait_recv()
+        all_got(k).wait_recv()
 
     def right_blocks(k, s):
         places = (cap + s, place_s[2 * s], place_s[2 * s + 1])
@@ -298,11 +313,7 @@
     for copy in near_d:
         copy.start()
 
-    @pl.loop(1, ROWS)
-    def _(step):
-        src = row_peer(step)
-        want_copy(src, r, src).wait_recv()
-
+    all_wants().wait_recv()
     to_smem = pltpu.make_async_copy(want_v, want_s, local_sem.at[5])
     to_smem.start()
     for load in loads[2:]:
@@ -345,13 +356,13 @@
 
     def row_copy(src, dst, peer):
         return pltpu.make_async_remote_copy(
-            src_ref=part, dst_ref=part_row.at[src], send_sem=row_send.at[dst], recv_sem=row_recv.at[src],
+            src_ref=part, dst_ref=part_row.at[src], send_sem=row_send, recv_sem=row_recv,
             device_id=(peer, c), device_id_type=MESH,
         )
 
     def col_copy(src, dst, peer):
         return pltpu.make_async_remote_copy(
-            src_ref=part_col.at[src], dst_ref=part_col.at[src], send_sem=col_send.at[dst], recv_sem=col_recv.at[src],
+            src_ref=part_col.at[src], dst_ref=part_col.at[src], send_sem=col_send, recv_sem=col_recv,
             device_id=(r, peer), device_id_type=MESH,
         )
 
@@ -366,11 +377,7 @@
         part_row[r] = part[...]
 
     def sum_cols_start():
-        @pl.loop(1, ROWS)
-        def _(step):
-            src = row_peer(step)
-            row_copy(src, r, src).wait_recv()
-
+        all_rows().wait_recv()
         part_col[c] = jnp.sum(part_row[...], axis=0)
 
         @pl.loop(1, COLS)
@@ -400,11 +407,7 @@
             part[3:4, :] += jnp.sum(turned_v[1, s] * back, axis=0, keepdims=True)
 
     def find_gamma():
-        @pl.loop(1, COLS)
-        def _(step):
-            src = col_peer(step)
-            col_copy(src, c, src).wait_recv()
-
+        all_cols().wait_recv()
         sums = jnp.sum(part_col[...], axis=0)
         over_ref[0, 0] = jnp.sum(sums[4:5, :])
         traces = jnp.sum(sums, axis=1, keepdims=True)
@@ -475,19 +478,11 @@
     for copy in (*near_d, *near_q, *table_copies, *mirror_copies):
         copy.wait_send()
 
-    @pl.loop(1, ROWS)
-    def _(step):
-        dst = row_peer(step)
-        want_copy(r, dst, dst).wait_send()
-        row_copy(r, dst, dst).wait_send()
-        for k in range(3):
-            deal_copy(k, r, dst, dst).wait_send()
-            got_copy(k, r, dst, dst).wait_send()
-
-    @pl.loop(1, COLS)
-    def _(step):
-        dst = col_peer(step)
-        col_copy(c, dst, dst).wait_send()
+    for copy in (all_wants(), all_rows(), all_cols()):
+        copy.wait_send()
+    for k in range(3):
+        all_dealt(k).wait_send()
+        all_got(k).wait_send()
 
 
 def step(cap, dealt, quick, collective_id, *operands):
@@ -536,16 +531,16 @@
             dma((9,)),
             dma((2, 2)),
             dma((2, 2)),
-            dma((3, ROWS)),
-            dma((3, ROWS)),
-            dma((3, ROWS)),
-            dma((3, ROWS)),
-            dma((ROWS,)),
-            dma((ROWS,)),
-            dma((ROWS,)),
-            dma((ROWS,)),
-            dma((COLS,)),
-            dma((COLS,)),
+            dma((3,)),
+            dma((3,)),
+            dma((3,)),
+            dma((3,)),
+            dma,
+            dma,
+            dma,
+            dma,
+            dma,
+            dma,
             dma((2,)),
             dma((2,)),
             dma((2,)),

time: 55.9 us -> 53.2 us (0.952)
  Pallas kernels: 53.4 us -> 50.7 us
    pallas_call x1, Pallas kernels: 52.3 us -> 49.6 us  [step(): pl.pallas_call(functools.partial(kernel, cap, dealt, quick), out_shape=(b...]
where the time goes in v6:
time: 53.2 us; the launch traced here: 53 us
  Pallas kernels  50.7 us (95%)
  between operations  1.47 us (3%)
  local copies, waits for them, and re-layouts  0.69 us (1%)
    pallas_call x1, Pallas kernels, step(): pl.pallas_call(functools.partial(kernel, cap, dealt, quick), out_shape=(b...  49.6 us
    pallas_call x1, Pallas kernels, write_out(): pl.pallas_call(write_kernel, out_shape=(block, block), in_specs=[any_spac...  1.07 us

profile of v6, /device:TPU:1, one launch (start us, length us, event | category | flops | bytes accessed | tf_op | source)
XLA Modules:
  0.0 53.0 jit_solution(3455982685985513378)
XLA Ops:
  0.6 0.0 copy-start.2
  0.6 0.0 copy-start.3
  0.7 0.7 %copy-done.2 = s32[1,10,3]{1,0,2:T(1,128)S(1)} copy-done((s32[1,10,3]{1,0,2:T(1,128)S(1)}, s32[1,10,3]{1,0,2:T(1,128)}, u32[]{:S(2)}) %copy-start.2) | copy-done | bytes 144
  1.3 0.0 copy-done.3
  1.3 0.0 copy-start
  1.3 0.0 copy-start.1
  1.3 49.6 %shard_map.59 = (f32[10,128,128]{2,1,0:T(8,128)S(1)}, f32[10,128,128]{2,1,0:T(8,128)S(1)}, f32[1,1]{1,0:T(1,128)}) custom-call(f32[10,128,128]{2,1,0:T(8,128)} %bitcast.7, f32[10,128,128]{2,1,0:T(8,128)} %bitcast.9, s32[3,1,10]{2,1,0:T(1,128)S(1)} %bitcast.13, s32[3,1,10]{2,1,0:T(1,128)S(1)} %bitcast.15), custom_call_target="tpu_custom_call" | custom-call | flops 1509949440 | bytes 819200 | tf_op jit(solution)/shard_map/pallas_call | solution.py:498
  51.6 0.0 copy-done
  51.6 0.0 copy-done.1
  51.6 0.2 conditional.1
  51.8 1.1 %shard_map.60 = (f32[10,128,128]{2,1,0:T(8,128)}, f32[10,128,128]{2,1,0:T(8,128)}) custom-call(f32[10,128,128]{2,1,0:T(8,128)S(1)} %get-tuple-element.30.new_in, f32[10,128,128]{2,1,0:T(8,128)S(1)} %get-tuple-element.31.ew_in), custom_call_target="tpu_custom_call" | custom-call | tf_op jit(solution)/shard_map/pallas_call | solution.py:568
Async XLA Ops:
  0.6 0.7 %copy-start.2 = (s32[1,10,3]{1,0,2:T(1,128)S(1)}, s32[1,10,3]{1,0,2:T(1,128)}, u32[]{:S(2)}) copy-start(s32[1,10,3]{1,0,2:T(1,128)} %param.10) | copy-start | bytes 364
  0.6 0.7 %copy-start.3 = (s32[1,10,3]{1,0,2:T(1,128)S(1)}, s32[1,10,3]{1,0,2:T(1,128)}, u32[]{:S(2)}) copy-start(s32[1,10,3]{1,0,2:T(1,128)} %param.11) | copy-start | bytes 364
  1.3 50.3 %copy-start = (f32[1,10,128,128]{3,2,1,0:T(8,128)S(1)}, f32[1,10,128,128]{3,2,1,0:T(8,128)}, u32[]{:S(2)}) copy-start(f32[1,10,128,128]{3,2,1,0:T(8,128)} %param.8) | copy-start | bytes 1966084
  1.3 50.3 %copy-start.1 = (f32[1,10,128,128]{3,2,1,0:T(8,128)S(1)}, f32[1,10,128,128]{3,2,1,0:T(8,128)}, u32[]{:S(2)}) copy-start(f32[1,10,128,128]{3,2,1,0:T(8,128)} %param.9) | copy-start | bytes 1966084

commit v7 on v6

--- a/solution.py
+++ b/solution.py
@@ -83,11 +83,11 @@
 
     barrier = pltpu.get_barrier_semaphore()
 
-    @pl.loop(1, ROWS)
+    @pl.loop(1, ROWS, unroll=True)
     def _(step):
         pl.semaphore_signal(barrier, inc=1, device_id=(row_peer(step), c), device_id_type=MESH)
 
-    @pl.loop(1, COLS)
+    @pl.loop(1, COLS, unroll=True)
     def _(step):
         pl.semaphore_signal(barrier, inc=1, device_id=(r, col_peer(step)), device_id_type=MESH)
 
@@ -205,7 +205,7 @@
         for p in range(dealt):
             pack[k, p] = own[slots[p]]
 
-        @pl.loop(1, ROWS)
+        @pl.loop(1, ROWS, unroll=True)
         def _(step):
             dst = row_peer(step)
             deal_copy(k, r, dst, dst).start()
@@ -303,7 +303,7 @@
         near = mirror_in[jnp.where(row == 2, 0, row * OFF_DIAG + table_s[row, 0, e])]
         return jnp.where(row == 2, got_d[:, place].reshape(BS, BS), near)
 
-    @pl.loop(1, ROWS)
+    @pl.loop(1, ROWS, unroll=True)
     def _(step):
         dst = row_peer(step)
         want_copy(r, dst, dst).start()
@@ -369,7 +369,7 @@
     def sum_rows_start():
         part[4:5, :] = jnp.zeros((1, BS), jnp.float32) + over
 
-        @pl.loop(1, ROWS)
+        @pl.loop(1, ROWS, unroll=True)
         def _(step):
             dst = row_peer(step)
             row_copy(r, dst, dst).start()
@@ -380,7 +380,7 @@
         all_rows().wait_recv()
         part_col[c] = jnp.sum(part_row[...], axis=0)
 
-        @pl.loop(1, COLS)
+        @pl.loop(1, COLS, unroll=True)
         def _(step):
             dst = col_peer(step)
             col_copy(c, dst, dst).start()

time: 53.2 us -> 52.8 us (level)
  no operation moved by 1% of the time
where the time goes in v7:
time: 52.8 us; the launch traced here: 52.7 us
  Pallas kernels  50.4 us (95%)
  between operations  1.47 us (3%)
  local copies, waits for them, and re-layouts  0.69 us (1%)
    pallas_call x1, Pallas kernels, step(): pl.pallas_call(functools.partial(kernel, cap, dealt, quick), out_shape=(b...  49.3 us
    pallas_call x1, Pallas kernels, write_out(): pl.pallas_call(write_kernel, out_shape=(block, block), in_specs=[any_spac...  1.07 us

profile of v7, /device:TPU:1, one launch (start us, length us, event | category | flops | bytes accessed | tf_op | source)
XLA Modules:
  0.0 52.7 jit_solution(3755229955258665444)
XLA Ops:
  0.6 0.0 copy-start.2
  0.6 0.0 copy-start.3
  0.7 0.7 %copy-done.2 = s32[1,10,3]{1,0,2:T(1,128)S(1)} copy-done((s32[1,10,3]{1,0,2:T(1,128)S(1)}, s32[1,10,3]{1,0,2:T(1,128)}, u32[]{:S(2)}) %copy-start.2) | copy-done | bytes 144
  1.3 0.0 copy-done.3
  1.3 0.0 copy-start
  1.3 0.0 copy-start.1
  1.3 49.3 %shard_map.59 = (f32[10,128,128]{2,1,0:T(8,128)S(1)}, f32[10,128,128]{2,1,0:T(8,128)S(1)}, f32[1,1]{1,0:T(1,128)}) custom-call(f32[10,128,128]{2,1,0:T(8,128)} %bitcast.7, f32[10,128,128]{2,1,0:T(8,128)} %bitcast.9, s32[3,1,10]{2,1,0:T(1,128)S(1)} %bitcast.13, s32[3,1,10]{2,1,0:T(1,128)S(1)} %bitcast.15), custom_call_target="tpu_custom_call" | custom-call | flops 1509949440 | bytes 819200 | tf_op jit(solution)/shard_map/pallas_call | solution.py:498
  51.3 0.0 copy-done
  51.3 0.0 copy-done.1
  51.3 0.2 conditional.1
  51.5 1.1 %shard_map.60 = (f32[10,128,128]{2,1,0:T(8,128)}, f32[10,128,128]{2,1,0:T(8,128)}) custom-call(f32[10,128,128]{2,1,0:T(8,128)S(1)} %get-tuple-element.30.new_in, f32[10,128,128]{2,1,0:T(8,128)S(1)} %get-tuple-element.31.ew_in), custom_call_target="tpu_custom_call" | custom-call | tf_op jit(solution)/shard_map/pallas_call | solution.py:568
Async XLA Ops:
  0.6 0.7 %copy-start.2 = (s32[1,10,3]{1,0,2:T(1,128)S(1)}, s32[1,10,3]{1,0,2:T(1,128)}, u32[]{:S(2)}) copy-start(s32[1,10,3]{1,0,2:T(1,128)} %param.10) | copy-start | bytes 364
  0.6 0.7 %copy-start.3 = (s32[1,10,3]{1,0,2:T(1,128)S(1)}, s32[1,10,3]{1,0,2:T(1,128)}, u32[]{:S(2)}) copy-start(s32[1,10,3]{1,0,2:T(1,128)} %param.11) | copy-start | bytes 364
  1.3 49.9 %copy-start = (f32[1,10,128,128]{3,2,1,0:T(8,128)S(1)}, f32[1,10,128,128]{3,2,1,0:T(8,128)}, u32[]{:S(2)}) copy-start(f32[1,10,128,128]{3,2,1,0:T(8,128)} %param.8) | copy-start | bytes 1966084
  1.3 49.9 %copy-start.1 = (f32[1,10,128,128]{3,2,1,0:T(8,128)S(1)}, f32[1,10,128,128]{3,2,1,0:T(8,128)}, u32[]{:S(2)}) copy-start(f32[1,10,128,128]{3,2,1,0:T(8,128)} %param.9) | copy-start | bytes 1966084

commit v8 on v7

--- a/solution.py
+++ b/solution.py
@@ -464,25 +464,17 @@
         sum_rows_start()
         sum_cols_start()
     gamma = find_gamma()
-    if EARLY == ROWS:
-        get_in(1)
-        make_energy()
-        get_in(2)
-        make_new(gamma)
-    else:
-        get_in(2)
-        make_new(gamma)
-        get_in(1)
-        make_energy()
-
-    for copy in (*near_d, *near_q, *table_copies, *mirror_copies):
-        copy.wait_send()
-
-    for copy in (all_wants(), all_rows(), all_cols()):
+    get_in(1)
+    make_energy()
+    for copy in (*near_d, *near_q, *table_copies, *mirror_copies, all_wants(), all_rows(), all_cols()):
         copy.wait_send()
     for k in range(3):
         all_dealt(k).wait_send()
+    for k in range(2):
         all_got(k).wait_send()
+    get_in(2)
+    make_new(gamma)
+    all_got(2).wait_send()
 
 
 def step(cap, dealt, quick, collective_id, *operands):

time: 52.8 us -> 52.8 us (level)
  no operation moved by 1% of the time
where the time goes in v8:
time: 52.8 us; the launch traced here: 52.7 us
  Pallas kernels  50.3 us (95%)
  between operations  1.47 us (3%)
  local copies, waits for them, and re-layouts  0.69 us (1%)
    pallas_call x1, Pallas kernels, step(): pl.pallas_call(functools.partial(kernel, cap, dealt, quick), out_shape=(b...  49.3 us
    pallas_call x1, Pallas kernels, write_out(): pl.pallas_call(write_kernel, out_shape=(block, block), in_specs=[any_spac...  1.07 us

profile of v8, /device:TPU:1, one launch (start us, length us, event | category | flops | bytes accessed | tf_op | source)
XLA Modules:
  0.0 52.7 jit_solution(11370397070411326020)
XLA Ops:
  0.6 0.0 copy-start.2
  0.6 0.0 copy-start.3
  0.7 0.7 %copy-done.2 = s32[1,10,3]{1,0,2:T(1,128)S(1)} copy-done((s32[1,10,3]{1,0,2:T(1,128)S(1)}, s32[1,10,3]{1,0,2:T(1,128)}, u32[]{:S(2)}) %copy-start.2) | copy-done | bytes 144
  1.3 0.0 copy-done.3
  1.3 0.0 copy-start
  1.3 0.0 copy-start.1
  1.3 49.3 %shard_map.59 = (f32[10,128,128]{2,1,0:T(8,128)S(1)}, f32[10,128,128]{2,1,0:T(8,128)S(1)}, f32[1,1]{1,0:T(1,128)}) custom-call(f32[10,128,128]{2,1,0:T(8,128)} %bitcast.7, f32[10,128,128]{2,1,0:T(8,128)} %bitcast.9, s32[3,1,10]{2,1,0:T(1,128)S(1)} %bitcast.13, s32[3,1,10]{2,1,0:T(1,128)S(1)} %bitcast.15), custom_call_target="tpu_custom_call" | custom-call | flops 1509949440 | bytes 819200 | tf_op jit(solution)/shard_map/pallas_call | solution.py:490
  51.2 0.0 copy-done
  51.3 0.0 copy-done.1
  51.3 0.2 conditional.1
  51.5 1.1 %shard_map.60 = (f32[10,128,128]{2,1,0:T(8,128)}, f32[10,128,128]{2,1,0:T(8,128)}) custom-call(f32[10,128,128]{2,1,0:T(8,128)S(1)} %get-tuple-element.30.new_in, f32[10,128,128]{2,1,0:T(8,128)S(1)} %get-tuple-element.31.ew_in), custom_call_target="tpu_custom_call" | custom-call | tf_op jit(solution)/shard_map/pallas_call | solution.py:560
Async XLA Ops:
  0.6 0.7 %copy-start.2 = (s32[1,10,3]{1,0,2:T(1,128)S(1)}, s32[1,10,3]{1,0,2:T(1,128)}, u32[]{:S(2)}) copy-start(s32[1,10,3]{1,0,2:T(1,128)} %param.10) | copy-start | bytes 364
  0.6 0.7 %copy-start.3 = (s32[1,10,3]{1,0,2:T(1,128)S(1)}, s32[1,10,3]{1,0,2:T(1,128)}, u32[]{:S(2)}) copy-start(s32[1,10,3]{1,0,2:T(1,128)} %param.11) | copy-start | bytes 364
  1.3 49.9 %copy-start = (f32[1,10,128,128]{3,2,1,0:T(8,128)S(1)}, f32[1,10,128,128]{3,2,1,0:T(8,128)}, u32[]{:S(2)}) copy-start(f32[1,10,128,128]{3,2,1,0:T(8,128)} %param.8) | copy-start | bytes 1966084
  1.3 49.9 %copy-start.1 = (f32[1,10,128,128]{3,2,1,0:T(8,128)S(1)}, f32[1,10,128,128]{3,2,1,0:T(8,128)}, u32[]{:S(2)}) copy-start(f32[1,10,128,128]{3,2,1,0:T(8,128)} %param.9) | copy-start | bytes 1966084
